TPU v7x, 32 devices: a whole 2x2x4 slice. The times are simulated.
32 devices in a mesh: grp: 2 (over core), dp: 16 (over z, y, x).
Axes of the slice: x: 2, y: 2, z: 4, core: 2. Of those that a mesh axis runs over, the one named last changes fastest.
Arguments:
- question_ids: int32 [512, 64], P(('grp', 'dp')), may hold values from 0 to 30719
- passage_ids: int32 [1024, 256], P(('grp', 'dp')), may hold values from 0 to 30719
- question_lengths: int32 [512], P(('grp', 'dp')), may hold values from 16 to 64
- passage_lengths: int32 [1024], P(('grp', 'dp')), may hold values from 64 to 256
- question_keys: int32 [512], P(('grp', 'dp')), may hold values from 0 to 15
- passage_keys: int32 [1024], P(('grp', 'dp')), may hold values from 0 to 15
- question_valid: int32 [512], P(('grp', 'dp')), may hold values 0 or 1
- word_table: float32 [2, 30720, 128], P('grp', 'dp'), may hold values from -0.3125 to 0.3125
- positions: float32 [2, 2, 256, 128], P('grp'), may hold values from -0.3125 to 0.3125
- attention: float32 [2, 2, 128, 512], P('grp'), may hold values from -0.5 to 0.5
- feedforward: float32 [2, 2, 2, 128, 512], P('grp'), may hold values from -0.5 to 0.5
- vectors: float32 [2, 2, 14, 128], P('grp'), as said below
- word_first: float32 [2, 30720, 128], P('grp', 'dp'), may hold values from -8.940697e-08 to 8.940697e-08
- positions_first: float32 [2, 2, 256, 128], P('grp'), may hold values from -3.33786e-06 to 3.33786e-06
- attention_first: float32 [2, 2, 128, 512], P('grp'), may hold values from -3.33786e-06 to 3.33786e-06
- feedforward_first: float32 [2, 2, 2, 128, 512], P('grp'), may hold values from -3.33786e-06 to 3.33786e-06
- vectors_first: float32 [2, 2, 14, 128], P('grp'), may hold values from -1.335144e-05 to 1.335144e-05
- word_second: float32 [2, 30720, 128], P('grp', 'dp'), may hold values from 1.0240082e-15 to 1.6384131e-14
- positions_second: float32 [2, 2, 256, 128], P('grp'), may hold values from 1.1377869e-14 to 1.820459e-13
- attention_second: float32 [2, 2, 128, 512], P('grp'), may hold values from 1.1377869e-14 to 1.820459e-13
- feedforward_second: float32 [2, 2, 2, 128, 512], P('grp'), may hold values from 1.1377869e-14 to 1.820459e-13
- vectors_second: float32 [2, 2, 14, 128], P('grp'), may hold values from 1.820459e-13 to 2.9127345e-12
- word_anchor: float32 [30720, 128], P('dp'), may hold values from -0.3125 to 0.3125
- positions_anchor: float32 [2, 256, 128], replicated, may hold values from -0.3125 to 0.3125
- attention_anchor: float32 [2, 128, 512], replicated, may hold values from -0.5 to 0.5
- feedforward_anchor: float32 [2, 2, 128, 512], replicated, may hold values from -0.5 to 0.5
- vectors_anchor: float32 [2, 14, 128], replicated, as said below
- word_outer: float32 [30720, 128], P('dp'), may hold values from -0.3125 to 0.3125
- positions_outer: float32 [2, 256, 128], replicated, may hold values from -0.3125 to 0.3125
- attention_outer: float32 [2, 128, 512], replicated, may hold values from -0.3125 to 0.3125
- feedforward_outer: float32 [2, 2, 128, 512], replicated, may hold values from -0.3125 to 0.3125
- vectors_outer: float32 [2, 14, 128], replicated, may hold values from -1.25 to 1.25
Outputs:
- loss_sum: float32 [2], P('grp')
- loss_count: float32 [2], P('grp')
- grad_norm: float32 [2], P('grp')
- word_first_next: float32 [2, 30720, 128], P('grp', 'dp')
- positions_first_next: float32 [2, 2, 256, 128], P('grp')
- attention_first_next: float32 [2, 2, 128, 512], P('grp')
- feedforward_first_next: float32 [2, 2, 2, 128, 512], P('grp')
- vectors_first_next: float32 [2, 2, 14, 128], P('grp')
- word_second_next: float32 [2, 30720, 128], P('grp', 'dp')
- positions_second_next: float32 [2, 2, 256, 128], P('grp')
- attention_second_next: float32 [2, 2, 128, 512], P('grp')
- feedforward_second_next: float32 [2, 2, 2, 128, 512], P('grp')
- vectors_second_next: float32 [2, 2, 14, 128], P('grp')
- word_average: float32 [30720, 128], P('dp')
- positions_average: float32 [2, 256, 128], replicated
- attention_average: float32 [2, 128, 512], replicated
- feedforward_average: float32 [2, 2, 128, 512], replicated
- vectors_average: float32 [2, 14, 128], replicated
- word_outer_next: float32 [30720, 128], P('dp')
- positions_outer_next: float32 [2, 256, 128], replicated
- attention_outer_next: float32 [2, 128, 512], replicated
- feedforward_outer_next: float32 [2, 2, 128, 512], replicated
- vectors_outer_next: float32 [2, 14, 128], replicated
- word_weight_next: float32 [2, 30720, 128], P('grp', 'dp')
- positions_weight_next: float32 [2, 2, 256, 128], P('grp')
- attention_weight_next: float32 [2, 2, 128, 512], P('grp')
- feedforward_weight_next: float32 [2, 2, 2, 128, 512], P('grp')
- vectors_weight_next: float32 [2, 2, 14, 128], P('grp')
Inputs may be any that keep to these rules, and one draw needn't show every extreme that they name: `vectors`: rows 0, 5 and 8 are norm gains near one, the others biases. `vectors_anchor`: rows 0, 5 and 8 are norm gains near one, the others biases.
All inputs are finite; a program needn't handle non-finite values. No bound on the sum of `question_valid` on one device may be relied on, other than what follows from the above.
Results may differ from a plain program's by a relative error of at most 0.018.
The roundings to bfloat16 on the way count: a program that leaves them out, or rounds other values in their place, can miss the bound.
Values may be sent and summed in bfloat16 or wider, within the bound.
A program may use at most 256 MiB of HBM per device.

v0:
```python
import functools
import math

import jax
import jax.numpy as jnp
from jax import lax
from jax.experimental import pallas as pl
from jax.experimental.pallas import tpu as pltpu
from jax.sharding import PartitionSpec as P

HEAD = 64
STEP = 5


NORM_EPS = 1e-05
MASKED = -1000000000.0
BETA_ONE = 0.9
BETA_TWO = 0.999
INNER_RATE = 0.05
WEIGHT_DECAY = 0.01
ADAM_EPS = 1e-08
CLIP_LIMIT = 0.01
OUTER_RATE = 0.7
OUTER_MU = 0.9
CONTRACT_ROWS = (((0,), (0,)), ((), ()))
CONTRACT_LAST = (((1,), (1,)), ((), ()))


def layer_norm(values, gain, shift):
    center = values - jnp.mean(values, -1, keepdims=True)
    spread = jnp.mean(center * center, -1, keepdims=True)
    return center * lax.rsqrt(spread + NORM_EPS) * gain + shift


def gelu_tanh(values):
    return jax.nn.gelu(values, approximate=True)


def low16(values):
    return values.astype(jnp.bfloat16)


NEG = -1e30
MESH = pl.DeviceIdType.MESH
VMEM_LIMIT = 60 * 1024 * 1024
WAYS = 4
SLOTS = 128
SPAN = WAYS * SLOTS
CHUNK = 256
RAW_Q = 64
RAW_FLAGS = 72
RAW_ROWS = 80


def enter(many):
    me = lax.axis_index("dp")
    barrier = pltpu.get_barrier_semaphore()

    def greet(step, carry):
        peer = lax.rem(me + step, many)
        pl.semaphore_signal(barrier, inc=1, device_id={"dp": peer}, device_id_type=MESH)
        return carry

    lax.fori_loop(1, many, greet, 0)
    pl.semaphore_wait(barrier, many - 1)
    return me


def copy_to(peer, src, dst, send, recv):
    return pltpu.make_async_remote_copy(
        src_ref=src,
        dst_ref=dst,
        send_sem=send,
        recv_sem=recv,
        device_id={"dp": peer},
        device_id_type=MESH,
    )


def spread_start(many, me, pairs, send, recv, slot):
    def step_start(step, carry):
        peer = lax.rem(me + step, many)
        for index, (source, landing) in enumerate(pairs):
            copy_to(
                peer,
                source(peer),
                landing.at[me],
                send.at[slot + index, peer],
                recv.at[slot + index, me],
            ).start()
        return carry

    lax.fori_loop(1, many, step_start, 0)


def spread_wait(many, me, pairs, send, recv, slot):
    def step_wait(step, carry):
        peer = lax.rem(me + step, many)
        for index, (source, landing) in enumerate(pairs):
            copy = copy_to(
                peer,
                source(peer),
                landing.at[peer],
                send.at[slot + index, peer],
                recv.at[slot + index, peer],
            )
            copy.wait_recv()
            copy.wait_send()
        return carry

    lax.fori_loop(1, many, step_wait, 0)


def dot(left, right):
    return jnp.dot(left, right, preferred_element_type=jnp.float32)


def dot_rows(left, right):
    return lax.dot_general(left, right, CONTRACT_ROWS, preferred_element_type=jnp.float32)


def dot_last(left, right):
    return lax.dot_general(left, right, CONTRACT_LAST, preferred_element_type=jnp.float32)


def iota(shape, axis):
    return lax.broadcasted_iota(jnp.int32, shape, axis)


def hot(mask):
    return jnp.where(mask, 1.0, 0.0).astype(jnp.bfloat16)


def rows_kernel(
    many, count_q, raw_ref, table_ref, every_ref, rows_ref, low_ref, offer, landed, own, send, recv
):
    me = enter(many)
    raw_pairs = [(lambda peer: raw_ref, every_ref)]
    spread_start(many, me, raw_pairs, send, recv, 0)
    every_ref[me] = raw_ref[...]
    depth = table_ref.shape[0]
    low_ref[...] = jnp.zeros_like(low_ref)
    low_ref[0:depth, :] = low16(table_ref[...])
    padded = low_ref.shape[0]
    spread_wait(many, me, raw_pairs, send, recv, 0)
    first = me * depth

    def pick(step, carry):
        peer = lax.rem(me + step, many)
        found = every_ref[peer].astype(jnp.int32)
        ask = jnp.concatenate(
            [
                found[RAW_Q : RAW_Q + count_q // 2, 0:1],
                found[RAW_Q : RAW_Q + count_q // 2, 64:65],
                found[0 : RAW_Q // 2, 0:1],
            ],
            0,
        )
        place = ask - first
        inside = (place >= 0) & (place < depth)
        spot = jnp.where(inside, place, -1)
        total = jnp.zeros((spot.shape[0], 128), jnp.float32)
        for cut in range(padded // CHUNK):
            wide = jnp.broadcast_to(spot, (spot.shape[0], CHUNK))
            chosen = hot(wide == iota(wide.shape, 1) + cut * CHUNK)
            total += dot(chosen, low_ref[cut * CHUNK : (cut + 1) * CHUNK, :])
        offer[peer] = low16(total)
        return carry

    lax.fori_loop(0, many, pick, 0)
    pairs = [(lambda peer: offer.at[peer], landed)]
    spread_start(many, me, pairs, send, recv, 1)
    landed[me] = offer[me]
    spread_wait(many, me, pairs, send, recv, 1)
    own[...] = low16(jnp.sum(landed[...].astype(jnp.float32), 0))
    pairs = [(lambda peer: own, rows_ref)]
    spread_start(many, me, pairs, send, recv, 2)
    rows_ref[me] = own[...]
    spread_wait(many, me, pairs, send, recv, 2)


def exchange_rows(many, count_q, count_p, raw, table):
    depth = table.shape[0]
    padded = -(-depth // CHUNK) * CHUNK
    both = count_q + count_p
    return pl.pallas_call(
        functools.partial(rows_kernel, many, count_q),
        out_shape=(
            jax.ShapeDtypeStruct((many, RAW_ROWS, 128), jnp.int16),
            jax.ShapeDtypeStruct((many, both, 128), jnp.bfloat16),
        ),
        in_specs=[pl.BlockSpec(memory_space=pltpu.VMEM)] * 2,
        out_specs=[pl.BlockSpec(memory_space=pltpu.VMEM)] * 2,
        scratch_shapes=[
            pltpu.VMEM((padded, 128), jnp.bfloat16),
            pltpu.VMEM((many, both, 128), jnp.bfloat16),
            pltpu.VMEM((many, both, 128), jnp.bfloat16),
            pltpu.VMEM((both, 128), jnp.bfloat16),
            pltpu.SemaphoreType.DMA((3, many)),
            pltpu.SemaphoreType.DMA((3, many)),
        ],
        compiler_params=pltpu.CompilerParams(
            collective_id=1, has_side_effects=True, vmem_limit_bytes=VMEM_LIMIT
        ),
        name="exchange_rows",
    )(raw, table)


def norm_rows(values, gain, shift):
    center = values - jnp.mean(values, -1, keepdims=True)
    spread = jnp.mean(center * center, -1, keepdims=True)
    return center * lax.rsqrt(spread + NORM_EPS) * gain + shift


def two_heads(values):
    lane = iota(values.shape, 1)
    low = jnp.where(lane < HEAD, values, jnp.zeros_like(values))
    high = jnp.where(lane >= HEAD, values, jnp.zeros_like(values))
    return jnp.concatenate([low, high], 0)


def merge_heads(both):
    half = both.shape[0] // 2
    lane = iota((half, both.shape[1]), 1)
    return jnp.where(lane < HEAD, both[:half], both[half:])


class Sizes:
    def __init__(self, many, count_q, count_p, depth):
        self.many = many
        self.count = (count_q, count_p)
        self.depth = depth
        self.padded = -(-depth // CHUNK) * CHUNK
        self.steps = (many // (2 * WAYS), many)
        self.spans = self.steps[0] + self.steps[1]
        self.devices = (2 * WAYS, 1)
        self.queries = (2 * WAYS * count_q, count_p)
        self.lines = 1024 // many
        self.kind = jnp.bfloat16 if self.lines % 16 == 0 else jnp.float32
        self.keep = self.spans * 136 * SPAN * 4 <= 8 * 1024 * 1024


def prepare_tokens(sizes, table_ref, place_ref, attn_ref, vec_ref, table_t, place_t, w_kv, vec_t):
    table_t[...] = jnp.zeros_like(table_t)
    depth = sizes.depth
    for cut in range(0, depth, 128):
        top = min(cut + 128, depth)
        piece = table_ref[cut:top, :]
        if top - cut < 128:
            piece = jnp.concatenate([piece, jnp.zeros((128 - (top - cut), 128), jnp.float32)], 0)
        table_t[:, cut : cut + 128] = low16(jnp.transpose(piece))
    for enc in range(2):
        place = place_ref[0, enc]
        for cut in range(0, place.shape[0], 128):
            turned = jnp.transpose(place[cut : cut + 128])
            high = low16(turned)
            place_t[enc, 0, :, cut : cut + 128] = high
            place_t[enc, 1, :, cut : cut + 128] = low16(turned - high.astype(jnp.float32))


def prepare_weights(attn_ref, vec_ref, w_kv, vec_t):
    for enc in range(2):
        for cut in range(2):
            w_kv[enc, cut * 128 : (cut + 1) * 128, :] = low16(
                jnp.transpose(attn_ref[0, enc, :, (cut + 1) * 128 : (cut + 2) * 128])
            )
        rows = jnp.concatenate(
            [vec_ref[0, enc, 0:10, :], jnp.zeros((118, 128), jnp.float32)], 0
        )
        vec_t[enc] = jnp.transpose(rows)


def lane_pick(values, lanes):
    return jnp.take_along_axis(values, lanes, axis=1, mode="promise_in_bounds")


def pack_span(sizes, enc, step, level, first, raw_ref, entries, counts):
    if enc == 1:
        ids = raw_ref[step, 0:RAW_Q, :].astype(jnp.int32)
    else:
        ids = jnp.concatenate(
            [
                raw_ref[step * 8 + i, RAW_Q:RAW_ROWS, :].astype(jnp.int32)[0:8]
                for i in range(8)
            ],
            0,
        )
    place = ids - first
    owned = (place >= 0) & (place < sizes.depth)
    flag = hot(owned)
    tall = iota((64, 64), 0)
    inside = dot(flag, hot(iota((128, 128), 0) <= iota((128, 128), 1)))
    total = dot(flag, jnp.ones((128, 128), jnp.bfloat16))
    before = dot(hot(iota((64, 64), 1) < tall), low16(total))
    counts[...] = jnp.maximum(counts[...], (before + total)[56:64])
    reached = (inside + before).astype(jnp.int32)
    start = before.astype(jnp.int32)
    stop = (before + total).astype(jnp.int32)
    line = iota((64, 128), 0)
    for window in range(WAYS):
        slot = iota((64, 128), 1) + (window * SLOTS + level * SPAN)
        lane = jnp.zeros((64, 128), jnp.int32)
        for jump in (64, 32, 16, 8, 4, 2, 1):
            seen = lane_pick(reached, lane + (jump - 1))
            lane = jnp.where(seen <= slot, lane + jump, lane)
        row = lane_pick(place, lane)
        if enc == 1:
            where = (line >> 5) * 128 + lane
            seq = (line & 31) + 1
        else:
            where = lane & 63
            seq = (line >> 3) * sizes.count[0] + (lane >> 6) * 8 + (line & 7) + 1
        code = (row << 16) + (where << 8) + seq
        code = jnp.where((slot >= start) & (slot < stop), code, 0)
        entries[0:1, window * SLOTS : (window + 1) * SLOTS] = jnp.sum(code, 0, keepdims=True)


def gather_span(sizes, enc, step, level, first, raw_ref, table_t, place_t, entries, counts, scaled_ref):
    pack_span(sizes, enc, step, level, first, raw_ref, entries, counts)
    code = entries[0:1, :]
    rows = code >> 16
    where = (code >> 8) & 255
    x = jnp.zeros((128, SPAN), jnp.float32)
    wide = jnp.broadcast_to(rows, (CHUNK, SPAN))
    for cut in range(sizes.padded // CHUNK):
        chosen = hot(wide == iota((CHUNK, SPAN), 0) + cut * CHUNK)
        x += dot(table_t[:, cut * CHUNK : (cut + 1) * CHUNK], chosen)
    chosen = hot(jnp.broadcast_to(where, (CHUNK, SPAN)) == iota((CHUNK, SPAN), 0))
    x += dot(place_t[enc, 0], chosen) + dot(place_t[enc, 1], chosen)
    center = x - jnp.mean(x, 0, keepdims=True)
    rate = lax.rsqrt(jnp.mean(center * center, 0, keepdims=True) + NORM_EPS)
    scaled_ref[0:128, :] = center * rate
    scaled_ref[128:129, :] = rate


def project(enc, scaled, vec_t, w_kv):
    a_t = low16(scaled * vec_t[enc, :, 0:1] + vec_t[enc, :, 1:2])
    kv = dot(w_kv[enc], a_t)
    keys_t = low16(kv[:128])
    values_t = low16(kv[128:] + vec_t[enc, :, 3:4])
    return a_t, keys_t, values_t


def forward_kernel(
    sizes,
    raw_ref,
    rows_ref,
    table_ref,
    place_ref,
    attn_ref,
    vec_ref,
    out_ref,
    lse_ref,
    query_ref,
    kept_ref,
    entry_ref,
    levels_ref,
    table_t,
    place_t,
    w_kv,
    vec_t,
    entries,
    counts,
    scaled_ref,
    query_q,
    total_q,
    top_q,
    mass_q,
    total_p,
    top_p,
    mass_p,
):
    first = lax.axis_index("dp") * sizes.depth
    count_q, count_p = sizes.count
    prepare_tokens(sizes, table_ref, place_ref, attn_ref, vec_ref, table_t, place_t, w_kv, vec_t)
    prepare_weights(attn_ref, vec_ref, w_kv, vec_t)
    counts[...] = jnp.zeros_like(counts)
    for enc in range(2):
        low, high = (0, count_q) if enc == 0 else (count_q, count_q + count_p)
        w_q = low16(attn_ref[0, enc, :, 0:128])

        def ask(step, carry):
            if enc == 0:
                held = jnp.concatenate(
                    [rows_ref[step * 8 + i, low:high, :] for i in range(8)], 0
                )
            else:
                held = rows_ref[step, low:high, :]
            x = held.astype(jnp.float32) + place_ref[0, enc, 0:1, :]
            h = norm_rows(x, vec_ref[0, enc, 0:1, :], vec_ref[0, enc, 1:2, :])
            query = low16(dot(low16(h), w_q) + vec_ref[0, enc, 2:3, :])
            if enc == 0:
                query_q[step] = query
                for i in range(8):
                    query_ref[step * 8 + i, low:high, :] = query[i * count_q : (i + 1) * count_q]
            else:
                query_ref[step, low:high, :] = query
            return carry

        lax.fori_loop(0, sizes.steps[enc], ask, 0)
    total_q[...] = jnp.zeros_like(total_q)
    total_p[...] = jnp.zeros_like(total_p)
    mass_q[...] = jnp.zeros_like(mass_q)
    mass_p[...] = jnp.zeros_like(mass_p)
    top_q[...] = jnp.full_like(top_q, NEG)
    top_p[...] = jnp.full_like(top_p, NEG)

    def one_level(state):
        level = state[0]
        for enc in range(2):
            total, top, mass = (total_q, top_q, mass_q) if enc == 0 else (total_p, top_p, mass_p)

            def one_span(step, carry):
                gather_span(
                    sizes, enc, step, level, first, raw_ref, table_t, place_t, entries, counts, scaled_ref
                )
                scaled = scaled_ref[0:128, :]
                if sizes.keep:
                    at = step if enc == 0 else sizes.steps[0] + step

                    @pl.when(level == 0)
                    def _():
                        kept_ref[at] = scaled_ref[...]
                        entry_ref[at] = entries[...]

                a_t, keys_t, values_t = project(enc, scaled, vec_t, w_kv)
                query = query_q[step] if enc == 0 else query_ref[step, count_q:, :]
                both = two_heads(query)
                number = query.shape[0]
                scores = dot(both, keys_t) * HEAD ** (-0.5)
                seq = (entries[0:1, :] & 255) - 1
                line = iota(scores.shape, 0)
                line = jnp.where(line >= number, line - number, line)
                mine = line == seq
                scores = jnp.where(mine, scores, NEG)
                old = top[step][:, 0:1]
                new = jnp.maximum(old, jnp.max(scores, 1, keepdims=True))
                fade = jnp.exp(old - new)
                expo = jnp.where(mine, jnp.exp(scores - new), 0.0)
                mass[step] = mass[step] * fade + jnp.sum(expo, 1, keepdims=True)
                top[step] = jnp.broadcast_to(new, top.shape[1:])
                mixed = dot_last(low16(expo), values_t)
                total[step] = total[step] * fade + mixed
                return carry

            lax.fori_loop(0, sizes.steps[enc], one_span, 0)
        need = (jnp.max(counts[...]).astype(jnp.int32) + SPAN - 1) // SPAN
        return level + 1, jnp.maximum(need, 1)

    last = lax.while_loop(lambda state: state[0] < state[1], one_level, (jnp.int32(0), jnp.int32(1)))
    levels_ref[0] = last[1]
    lse_ref[...] = jnp.full_like(lse_ref, NEG)
    for enc in range(2):
        total, top, mass = (total_q, top_q, mass_q) if enc == 0 else (total_p, top_p, mass_p)

        def close(step, carry):
            bulk = mass[step]
            some = bulk > 0.0
            safe = jnp.where(some, bulk, 1.0)
            mixed = merge_heads(total[step] / safe)
            lse = jnp.where(some, top[step] + jnp.log(safe), NEG)
            if enc == 1:
                out_ref[step, count_q:, :] = low16(mixed)
                tall = jnp.concatenate([lse, jnp.full((128 - 2 * count_p, 128), NEG, jnp.float32)], 0)
                lse_ref[step, 0:1, :] = jnp.transpose(tall)[0:1, :]
            else:
                half = lse.shape[0] // 2
                for i in range(8):
                    out_ref[step * 8 + i, 0:count_q, :] = low16(mixed[i * count_q : (i + 1) * count_q])
                    tall = jnp.concatenate(
                        [
                            lse[i * count_q : (i + 1) * count_q],
                            lse[half + i * count_q : half + (i + 1) * count_q],
                            jnp.full((128 - 2 * count_q, 128), NEG, jnp.float32),
                        ],
                        0,
                    )
                    lse_ref[step * 8 + i, 1:2, :] = jnp.transpose(tall)[0:1, :]
            return carry

        lax.fori_loop(0, sizes.steps[enc], close, 0)


def token_scratch(sizes):
    return [
        pltpu.VMEM((128, sizes.padded), jnp.bfloat16),
        pltpu.VMEM((2, 2, 128, CHUNK), jnp.bfloat16),
        pltpu.VMEM((2, 256, 128), jnp.bfloat16),
        pltpu.VMEM((2, 128, 128), jnp.float32),
        pltpu.VMEM((8, SPAN), jnp.int32),
        pltpu.VMEM((8, 128), jnp.float32),
        pltpu.VMEM((136, SPAN), jnp.float32),
    ]


def local_call(kernel, out_shape, inputs, scratch, name, smem_in=(), smem_out=()):
    vm = pl.BlockSpec(memory_space=pltpu.VMEM)
    sm = pl.BlockSpec(memory_space=pltpu.SMEM)
    return pl.pallas_call(
        kernel,
        out_shape=out_shape,
        in_specs=[sm if i in smem_in else vm for i in range(len(inputs))],
        out_specs=[sm if i in smem_out else vm for i in range(len(out_shape))],
        scratch_shapes=scratch,
        compiler_params=pltpu.CompilerParams(vmem_limit_bytes=VMEM_LIMIT),
        name=name,
    )(*inputs)


def tokens_forward(sizes, every, rows, table, positions, attention, vectors):
    many = sizes.many
    both = sum(sizes.count)
    kept = sizes.spans if sizes.keep else 1
    state = []
    for enc in range(2):
        tall = 2 * sizes.queries[enc]
        state += [pltpu.VMEM((sizes.steps[enc], tall, 128), jnp.float32)] * 3
    return local_call(
        functools.partial(forward_kernel, sizes),
        (
            jax.ShapeDtypeStruct((many, both, 128), jnp.bfloat16),
            jax.ShapeDtypeStruct((many, 8, 128), jnp.float32),
            jax.ShapeDtypeStruct((many, both, 128), jnp.bfloat16),
            jax.ShapeDtypeStruct((kept, 136, SPAN), jnp.float32),
            jax.ShapeDtypeStruct((kept, 8, SPAN), jnp.int32),
            jax.ShapeDtypeStruct((1,), jnp.int32),
        ),
        (every, rows, table, positions, attention, vectors),
        token_scratch(sizes)
        + [pltpu.VMEM((sizes.steps[0], sizes.queries[0], 128), jnp.bfloat16)]
        + state,
        "tokens_forward",
        smem_out=(5,),
    )


def mix_kernel(
    many, count_q, part_ref, lse_ref, mixed_ref, total_ref, landed, landed_lse, own, own_lse, send, recv
):
    me = enter(many)
    pairs = [
        (lambda peer: part_ref.at[peer], landed),
        (lambda peer: lse_ref.at[peer], landed_lse),
    ]
    spread_start(many, me, pairs, send, recv, 0)
    landed[me] = part_ref[me]
    landed_lse[me] = lse_ref[me]
    spread_wait(many, me, pairs, send, recv, 0)
    parts = landed_lse[...]
    top = jnp.max(parts, 0)
    total = top + jnp.log(jnp.sum(jnp.exp(parts - top[None]), 0))
    own_lse[...] = total
    share = jnp.exp(parts - total[None])
    columns = jnp.transpose(share.reshape(many * 8, 128))
    count_p = part_ref.shape[1] - count_q
    mixed = jnp.zeros((count_q + count_p, 128), jnp.float32)
    lane_q = iota((count_q, 128), 1)
    lane_p = iota((count_p, 128), 1)
    for peer in range(many):
        factor_p = jnp.where(
            lane_p < HEAD,
            columns[0:count_p, peer * 8 : peer * 8 + 1],
            columns[count_p : 2 * count_p, peer * 8 : peer * 8 + 1],
        )
        factor_q = jnp.where(
            lane_q < HEAD,
            columns[0:count_q, peer * 8 + 1 : peer * 8 + 2],
            columns[count_q : 2 * count_q, peer * 8 + 1 : peer * 8 + 2],
        )
        mixed += jnp.concatenate([factor_q, factor_p], 0) * landed[peer].astype(jnp.float32)
    own[...] = low16(mixed)
    pairs = [(lambda peer: own, mixed_ref), (lambda peer: own_lse, total_ref)]
    spread_start(many, me, pairs, send, recv, 2)
    mixed_ref[me] = own[...]
    total_ref[me] = own_lse[...]
    spread_wait(many, me, pairs, send, recv, 2)


def remote_call(kernel, out_shape, inputs, scratch, lanes, many, ident, name):
    return pl.pallas_call(
        kernel,
        out_shape=out_shape,
        in_specs=[pl.BlockSpec(memory_space=pltpu.VMEM)] * len(inputs),
        out_specs=[pl.BlockSpec(memory_space=pltpu.VMEM)] * len(out_shape),
        scratch_shapes=scratch
        + [pltpu.SemaphoreType.DMA((lanes, many)), pltpu.SemaphoreType.DMA((lanes, many))],
        compiler_params=pltpu.CompilerParams(
            collective_id=ident, has_side_effects=True, vmem_limit_bytes=VMEM_LIMIT
        ),
        name=name,
    )(*inputs)


def exchange_mixed(sizes, part, lse):
    many = sizes.many
    both = sum(sizes.count)
    return remote_call(
        functools.partial(mix_kernel, many, sizes.count[0]),
        (
            jax.ShapeDtypeStruct((many, both, 128), jnp.bfloat16),
            jax.ShapeDtypeStruct((many, 8, 128), jnp.float32),
        ),
        (part, lse),
        [
            pltpu.VMEM((many, both, 128), jnp.bfloat16),
            pltpu.VMEM((many, 8, 128), jnp.float32),
            pltpu.VMEM((both, 128), jnp.bfloat16),
            pltpu.VMEM((8, 128), jnp.float32),
        ],
        4,
        many,
        2,
        "exchange_mixed",
    )


def backward_kernel(
    sizes,
    levels_ref,
    raw_ref,
    query_ref,
    mixed_ref,
    lse_ref,
    grad_ref,
    kept_ref,
    entry_ref,
    table_ref,
    place_ref,
    attn_ref,
    vec_ref,
    d_query_ref,
    d_table_ref,
    slice_ref,
    d_vec_ref,
    table_t,
    place_t,
    w_kv,
    vec_t,
    entries,
    counts,
    scaled_ref,
    d_place_ref,
    d_attn_ref,
    acc_gain,
    acc_shift,
    acc_value,
    d_query_q,
    d_query_p,
):
    first = lax.axis_index("dp") * sizes.depth
    count_q, count_p = sizes.count
    prepare_weights(attn_ref, vec_ref, w_kv, vec_t)
    again = levels_ref[0] > 1 if sizes.keep else levels_ref[0] > 0

    @pl.when(again)
    def _():
        prepare_tokens(sizes, table_ref, place_ref, attn_ref, vec_ref, table_t, place_t, w_kv, vec_t)

    counts[...] = jnp.zeros_like(counts)
    d_table_ref[...] = jnp.zeros_like(d_table_ref)
    d_place_ref[...] = jnp.zeros_like(d_place_ref)
    d_attn_ref[...] = jnp.zeros_like(d_attn_ref)
    d_query_p[...] = jnp.zeros_like(d_query_p)
    d_query_q[...] = jnp.zeros_like(d_query_q)
    acc_gain[...] = jnp.zeros_like(acc_gain)
    acc_shift[...] = jnp.zeros_like(acc_shift)
    acc_value[...] = jnp.zeros_like(acc_value)

    def one_level(level, carry_level):
        for enc in range(2):
            w_all = low16(attn_ref[0, enc, :, 128:384])

            def one_span(step, carry):
                at = step if enc == 0 else sizes.steps[0] + step
                again_span = functools.partial(
                    gather_span, sizes, enc, step, level, first, raw_ref, table_t, place_t, entries, counts, scaled_ref
                )
                if sizes.keep:

                    @pl.when(level == 0)
                    def _():
                        scaled_ref[...] = kept_ref[at]
                        entries[...] = entry_ref[at]

                    pl.when(level > 0)(again_span)
                else:
                    again_span()
                scaled = scaled_ref[0:128, :]
                a_t, keys_t, values_t = project(enc, scaled, vec_t, w_kv)
                if enc == 0:
                    query = jnp.concatenate([query_ref[step * 8 + i, 0:count_q, :] for i in range(8)], 0)
                    grad = jnp.concatenate([grad_ref[step * 8 + i, 0:count_q, :] for i in range(8)], 0)
                    mixed = jnp.concatenate([mixed_ref[step * 8 + i, 0:count_q, :] for i in range(8)], 0)
                    pieces = []
                    for head in range(2):
                        for i in range(8):
                            line = lse_ref[step * 8 + i]
                            tall = jnp.transpose(
                                jnp.concatenate([line, jnp.zeros((120, 128), jnp.float32)], 0)
                            )
                            pieces.append(tall[head * count_q : (head + 1) * count_q, 1:2])
                    lse = jnp.concatenate(pieces, 0)
                else:
                    query = query_ref[step, count_q:, :]
                    grad = grad_ref[step, count_q:, :]
                    mixed = mixed_ref[step, count_q:, :]
                    tall = jnp.transpose(
                        jnp.concatenate([lse_ref[step], jnp.zeros((120, 128), jnp.float32)], 0)
                    )
                    lse = tall[0 : 2 * count_p, 0:1]
                number = query.shape[0]
                both = two_heads(query)
                grads = two_heads(grad)
                level_sum = jnp.sum(
                    grads.astype(jnp.float32) * jnp.concatenate([mixed, mixed], 0).astype(jnp.float32),
                    1,
                    keepdims=True,
                )
                scores = dot(both, keys_t) * HEAD ** (-0.5)
                seq = (entries[0:1, :] & 255) - 1
                line = iota(scores.shape, 0)
                line = jnp.where(line >= number, line - number, line)
                mine = line == seq
                probs = jnp.where(mine, jnp.exp(jnp.where(mine, scores, NEG) - lse), 0.0)
                d_probs = dot(grads, values_t)
                d_scores = low16(probs * (d_probs - level_sum))
                d_values = low16(dot_rows(grads, low16(probs)))
                d_keys = low16(dot_rows(both, d_scores) * HEAD ** (-0.5))
                d_query = merge_heads(dot_last(d_scores, keys_t)) * HEAD ** (-0.5)
                if enc == 0:
                    d_query_q[step] += d_query
                else:
                    d_query_p[step] += d_query
                d_kv = jnp.concatenate([d_keys, d_values], 0)
                d_attn_ref[enc] += dot_last(a_t, d_kv)
                acc_value[enc] += d_values.astype(jnp.float32)
                d_h = dot(w_all, d_kv)
                acc_gain[enc] += d_h * scaled
                acc_shift[enc] += d_h
                d_scaled = d_h * vec_t[enc, :, 0:1]
                center = d_scaled - jnp.mean(d_scaled, 0, keepdims=True)
                slope = jnp.mean(d_scaled * scaled, 0, keepdims=True)
                d_x = low16((center - scaled * slope) * scaled_ref[128:129, :])
                rows = entries[0:1, :] >> 16
                where = (entries[0:1, :] >> 8) & 255
                chosen = hot(jnp.broadcast_to(where, (CHUNK, SPAN)) == iota((CHUNK, SPAN), 0))
                d_place_ref[enc] += dot_last(d_x, chosen)
                wide = jnp.broadcast_to(rows, (CHUNK, SPAN))
                for cut in range(sizes.padded // CHUNK):
                    spot = slice(cut * CHUNK, (cut + 1) * CHUNK)
                    chosen = hot(wide == iota((CHUNK, SPAN), 0) + cut * CHUNK)
                    d_table_ref[:, spot] += dot_last(d_x, chosen)
                return carry

            lax.fori_loop(0, sizes.steps[enc], one_span, 0)
        return carry_level

    lax.fori_loop(0, levels_ref[0], one_level, 0)

    def give(step, carry):
        for i in range(8):
            d_query_ref[step * 8 + i, 0:count_q, :] = low16(
                d_query_q[step][i * count_q : (i + 1) * count_q]
            )
        return carry

    lax.fori_loop(0, sizes.steps[0], give, 0)
    d_query_ref[:, count_q:, :] = low16(d_query_p[...])
    for enc in range(2):
        for part, block in enumerate((d_place_ref, d_attn_ref)):
            for cut in range(2):
                slice_ref[enc, 2 * part + cut] = block[enc, :, cut * 128 : (cut + 1) * 128].astype(
                    slice_ref.dtype
                )
    d_vec_ref[...] = jnp.zeros_like(d_vec_ref)
    for enc in range(2):
        for row, acc in enumerate((acc_gain, acc_shift, acc_value)):
            tall = jnp.broadcast_to(jnp.sum(acc[enc], 1, keepdims=True), (128, 128))
            d_vec_ref[enc * 4 + row : enc * 4 + row + 1, :] = jnp.transpose(tall)[0:1, :]


def tokens_backward(sizes, levels, every, query, mixed, lse, grad, kept, entry, table, positions, attention, vectors):
    many = sizes.many
    count_p = sizes.count[1]
    both = sum(sizes.count)
    return local_call(
        functools.partial(backward_kernel, sizes),
        (
            jax.ShapeDtypeStruct((many, both, 128), jnp.bfloat16),
            jax.ShapeDtypeStruct((128, sizes.padded), jnp.float32),
            jax.ShapeDtypeStruct((2, 4, 128, 128), sizes.kind),
            jax.ShapeDtypeStruct((8, 128), jnp.float32),
        ),
        (levels, every, query, mixed, lse, grad, kept, entry, table, positions, attention, vectors),
        token_scratch(sizes)
        + [
            pltpu.VMEM((2, 128, CHUNK), jnp.float32),
            pltpu.VMEM((2, 128, 256), jnp.float32),
            pltpu.VMEM((2, 128, SPAN), jnp.float32),
            pltpu.VMEM((2, 128, SPAN), jnp.float32),
            pltpu.VMEM((2, 128, SPAN), jnp.float32),
            pltpu.VMEM((sizes.steps[0], sizes.queries[0], 128), jnp.float32),
            pltpu.VMEM((many, count_p, 128), jnp.float32),
        ],
        "tokens_backward",
        smem_in=(0,),
    )


def adam(weight, grad, first, second):
    first_new = BETA_ONE * first + (1.0 - BETA_ONE) * grad
    second_new = BETA_TWO * second + (1.0 - BETA_TWO) * grad * grad
    fix_one = 1.0 - BETA_ONE**STEP
    fix_two = 1.0 - BETA_TWO**STEP
    ratio = first_new / fix_one / (jnp.sqrt(second_new / fix_two) + ADAM_EPS)
    return (first_new, second_new, weight - INNER_RATE * (ratio + WEIGHT_DECAY * weight))


def pieces_of(depth):
    blocks = [(1, (enc,)) for enc in range(2)] + [(2, (enc,)) for enc in range(2)]
    blocks += [(3, (enc, side)) for enc in range(2) for side in range(2)]
    blocks += [(4, (enc,)) for enc in range(2)]
    return blocks


def square_sum(values):
    return jnp.sum(jnp.sum(values * values, 0, keepdims=True), 1, keepdims=True)


def finish_kernel(sizes, *refs):
    many = sizes.many
    count_q, count_p = sizes.count
    depth = sizes.depth
    (query_ref, slice_ref, first_ref, d_table_ref, rows_ref, raw_ref, xa_q, xa_p, d_out, d_ffn, d_mid) = refs[:11]
    place_ref, attn_ref, vec_ref = refs[11:14]
    state = refs[14:34]
    norm_ref, g_word, g_place, g_attn, g_vec = refs[34:39]
    theirs = refs[39:44]
    held = refs[44:64]
    mine = refs[64:69]
    (query_all, slice_all, first_all, scalar_all, land_query, land_slice, own_query, own_slice, tile, table_t) = refs[69:79]
    send, recv, load, pair_send, pair_recv = refs[79:84]
    loads = []
    for index in range(20):
        copy = pltpu.make_async_copy(state[index], held[index], load.at[index])
        copy.start()
        loads.append(copy)
    me = lax.axis_index("dp")
    other = 1 - lax.axis_index("grp")
    barrier = pltpu.get_barrier_semaphore()

    def greet(step, carry):
        peer = lax.rem(me + step, many)
        pl.semaphore_signal(barrier, inc=1, device_id={"dp": peer}, device_id_type=MESH)
        return carry

    lax.fori_loop(1, many, greet, 0)
    pl.semaphore_signal(barrier, inc=1, device_id={"grp": other}, device_id_type=MESH)
    pl.semaphore_wait(barrier, many)
    pairs = [
        (lambda peer: query_ref.at[peer], land_query),
        (lambda peer: slice_ref.at[peer], land_slice),
        (lambda peer: first_ref, first_all),
    ]
    spread_start(many, me, pairs, send, recv, 0)
    land_query[me] = query_ref[me]
    land_slice[me] = slice_ref[me]
    first_all[me] = first_ref[...]
    spread_wait(many, me, pairs, send, recv, 0)
    own_query[...] = low16(jnp.sum(land_query[...].astype(jnp.float32), 0))
    own_slice[...] = jnp.sum(land_slice[...].astype(jnp.float32), 0).astype(own_slice.dtype)
    pairs = [(lambda peer: own_query, query_all), (lambda peer: own_slice, slice_all)]
    spread_start(many, me, pairs, send, recv, 3)
    query_all[me] = own_query[...]
    slice_all[me] = own_slice[...]
    spread_wait(many, me, pairs, send, recv, 3)

    first_sum = jnp.sum(first_all[...], 0)
    first = me * depth
    table_t[...] = d_table_ref[...]
    blocks = slice_all[...].astype(jnp.float32).reshape(8, 128, 128)
    rest = jnp.zeros((1, 1), jnp.float32)
    for enc in range(2):
        low, high = (0, count_q) if enc == 0 else (count_q, count_q + count_p)
        number = many * (high - low)
        d_query = query_all[:, low:high, :].reshape(number, 128)
        x = rows_ref[:, low:high, :].reshape(number, 128).astype(jnp.float32) + place_ref[0, enc, 0:1, :]
        center = x - jnp.mean(x, -1, keepdims=True)
        rate = lax.rsqrt(jnp.mean(center * center, -1, keepdims=True) + NORM_EPS)
        scaled = center * rate
        gain = vec_ref[0, enc, 0:1, :]
        a_low = low16(scaled * gain + vec_ref[0, enc, 1:2, :])
        xa = xa_q if enc == 0 else xa_p
        d_h = xa[...] + dot_last(d_query, low16(attn_ref[0, enc, :, 0:128]))
        d_scaled = d_h * gain
        slope = jnp.mean(d_scaled * scaled, -1, keepdims=True)
        d_x = (d_scaled - jnp.mean(d_scaled, -1, keepdims=True) - scaled * slope) * rate
        g_place[enc, 0:128, :] = jnp.transpose(blocks[enc * 4])
        g_place[enc, 128:256, :] = jnp.transpose(blocks[enc * 4 + 1])
        g_place[enc, 0:1, :] += jnp.sum(d_x, 0, keepdims=True)
        g_attn[enc, :, 0:128] = dot_rows(a_low, d_query)
        g_attn[enc, :, 128:256] = blocks[enc * 4 + 2]
        g_attn[enc, :, 256:384] = blocks[enc * 4 + 3]
        g_attn[enc, :, 384:512] = d_out[enc]
        g_vec[enc] = d_mid[enc]
        g_vec[enc, 0:1, :] = first_sum[enc * 4 : enc * 4 + 1] + jnp.sum(d_h * scaled, 0, keepdims=True)
        g_vec[enc, 1:2, :] = first_sum[enc * 4 + 1 : enc * 4 + 2] + jnp.sum(d_h, 0, keepdims=True)
        g_vec[enc, 2:3, :] = jnp.sum(d_query.astype(jnp.float32), 0, keepdims=True)
        g_vec[enc, 3:4, :] = first_sum[enc * 4 + 2 : enc * 4 + 3]
        if enc == 0:
            columns = [
                part
                for peer in range(many)
                for part in (
                    raw_ref[peer, RAW_Q : RAW_Q + 16, 0:1].astype(jnp.int32)[0 : count_q // 2],
                    raw_ref[peer, RAW_Q : RAW_Q + 16, 64:65].astype(jnp.int32)[0 : count_q // 2],
                )
            ]
        else:
            columns = [raw_ref[peer, 0:count_p, 0:1].astype(jnp.int32) for peer in range(many)]
        spot = jnp.concatenate(columns, 0) - first
        spot = jnp.where(spot < depth, spot, -1)
        d_low = low16(d_x)
        wide = jnp.broadcast_to(spot, (number, CHUNK))
        for cut in range(sizes.padded // CHUNK):
            chosen = hot(wide == iota((number, CHUNK), 1) + cut * CHUNK)
            table_t[:, cut * CHUNK : (cut + 1) * CHUNK] += dot_rows(d_low, chosen)
        rest += square_sum(g_place[enc]) + square_sum(g_attn[enc]) + square_sum(g_vec[enc])
        rest += square_sum(d_ffn[enc, 0]) + square_sum(d_ffn[enc, 1])
    for cut in range(0, depth, 128):
        top = min(cut + 128, depth)
        g_word[cut:top, :] = jnp.transpose(table_t[:, cut : cut + 128])[0 : top - cut]
    tile[...] = jnp.broadcast_to(square_sum(table_t[...]), (8, 128))
    pairs = [(lambda peer: tile, scalar_all)]
    spread_start(many, me, pairs, send, recv, 5)
    scalar_all[me] = tile[...]
    for copy in loads:
        copy.wait()
    spread_wait(many, me, pairs, send, recv, 5)
    norm = jnp.sqrt(jnp.sum(scalar_all[...], 0)[0:1, 0:1] + rest)
    norm_ref[...] = jnp.broadcast_to(norm, (8, 128))
    factor = CLIP_LIMIT / jnp.maximum(norm, CLIP_LIMIT)
    grads = (g_word, g_place, g_attn, d_ffn, g_vec)

    def differ(kind, at, rows):
        weight, moment, square, anchor = (held[kind * 4 + j] for j in range(4))
        grad = grads[kind][at + (rows,)] * factor
        inner = adam(weight[(0,) + at + (rows,)], grad, moment[(0,) + at + (rows,)], square[(0,) + at + (rows,)])[2]
        mine[kind][at + (rows,)] = anchor[at + (rows,)] - inner

    size = math.gcd(depth, 128)

    def table_block(step, carry):
        differ(0, (), pl.ds(pl.multiple_of(step * size, size), size))
        return carry

    lax.fori_loop(0, depth // size, table_block, 0)
    ways = []

    def hand(kind):
        copy = pltpu.make_async_remote_copy(
            src_ref=mine[kind],
            dst_ref=theirs[kind],
            send_sem=pair_send.at[kind],
            recv_sem=pair_recv.at[kind],
            device_id={"grp": other},
            device_id_type=MESH,
        )
        copy.start()
        ways.append(copy)

    hand(0)
    for kind in range(1, 5):
        for found, at in pieces_of(depth):
            if found == kind:
                differ(kind, at, slice(0, 14) if kind == 4 else slice(None))
        hand(kind)
    for kind in range(5):
        ways[kind].wait()


    def table_add(step, carry):
        rows = pl.ds(pl.multiple_of(step * size, size), size)
        theirs[0][rows] += mine[0][rows]
        return carry

    lax.fori_loop(0, depth // size, table_add, 0)
    for kind, at in pieces_of(depth):
        theirs[kind][at] += mine[kind][at]


def finish(sizes, query, slices, first, d_table, rows, every, xa_q, xa_p, d_out, d_ffn, d_mid, params, state):
    many = sizes.many
    both = sum(sizes.count)
    inputs = (query, slices, first, d_table, rows, every, xa_q, xa_p, d_out, d_ffn, d_mid) + params
    flat = tuple(state[j][kind] for kind in range(5) for j in range(4))
    shapes = [state[3][kind].shape for kind in range(5)]
    vm = pl.BlockSpec(memory_space=pltpu.VMEM)
    hbm = pl.BlockSpec(memory_space=pl.ANY)
    f32 = jnp.float32
    return pl.pallas_call(
        functools.partial(finish_kernel, sizes),
        out_shape=tuple(
            jax.ShapeDtypeStruct(shape, f32)
            for shape in [(8, 128), shapes[0], shapes[1], shapes[2], (2, 16, 128)] + shapes
        ),
        in_specs=[vm] * len(inputs) + [hbm] * 20,
        out_specs=[vm] * 10,
        scratch_shapes=[pltpu.VMEM(value.shape, f32) for value in flat]
        + [pltpu.VMEM(shape, f32) for shape in shapes]
        + [
            pltpu.VMEM((many, both, 128), jnp.bfloat16),
            pltpu.VMEM((many, sizes.lines, 128), sizes.kind),
            pltpu.VMEM((many, 8, 128), f32),
            pltpu.VMEM((many, 8, 128), f32),
            pltpu.VMEM((many, both, 128), jnp.bfloat16),
            pltpu.VMEM((many, sizes.lines, 128), sizes.kind),
            pltpu.VMEM((both, 128), jnp.bfloat16),
            pltpu.VMEM((sizes.lines, 128), sizes.kind),
            pltpu.VMEM((8, 128), f32),
            pltpu.VMEM((128, sizes.padded), f32),
            pltpu.SemaphoreType.DMA((6, many)),
            pltpu.SemaphoreType.DMA((6, many)),
            pltpu.SemaphoreType.DMA((20,)),
            pltpu.SemaphoreType.DMA((5,)),
            pltpu.SemaphoreType.DMA((5,)),
        ],
        compiler_params=pltpu.CompilerParams(
            collective_id=3, has_side_effects=True, vmem_limit_bytes=VMEM_LIMIT
        ),
        name="finish",
    )(*inputs, *flat)


def outputs_kernel(depth, groups, *refs):
    norm_ref, g_vec = refs[:2]
    ins = refs[2:31]
    outs = refs[31:56]
    held = refs[56:85]
    made = refs[85:110]
    load, store = refs[110:112]
    loads, stores = ([], [])
    for index in range(29):
        copy = pltpu.make_async_copy(ins[index], held[index], load.at[index])
        copy.start()
        loads.append(copy)
    norm = norm_ref[0:1, 0:1]
    factor = CLIP_LIMIT / jnp.maximum(norm, CLIP_LIMIT)
    grads = tuple(held[25:29]) + (g_vec,)

    def work(kind, at, rows):
        moment, square, anchor, outer, summed = (held[kind * 5 + j] for j in range(5))
        first, second, average, momentum, weight = (made[kind * 5 + j] for j in range(5))
        spot = at + (rows,)
        deep = (0,) + spot
        grad = grads[kind][spot] * factor
        first[deep] = BETA_ONE * moment[deep] + (1.0 - BETA_ONE) * grad
        second[deep] = BETA_TWO * square[deep] + (1.0 - BETA_TWO) * grad * grad
        mean = summed[spot] / groups
        speed = OUTER_MU * outer[spot] + mean
        average[spot] = mean
        momentum[spot] = speed
        weight[deep] = anchor[spot] - OUTER_RATE * (mean + OUTER_MU * speed)

    def give(kind):
        for j in range(5):
            index = kind * 5 + j
            copy = pltpu.make_async_copy(made[index], outs[index], store.at[index])
            copy.start()
            stores.append(copy)

    size = math.gcd(depth, 128)

    def table_block(step, carry):
        work(0, (), pl.ds(pl.multiple_of(step * size, size), size))
        return carry

    for kind in range(5):
        for j in range(5):
            loads[kind * 5 + j].wait()
        if kind < 4:
            loads[25 + kind].wait()
        if kind == 0:
            lax.fori_loop(0, depth // size, table_block, 0)
        else:
            for found, at in pieces_of(depth):
                if found == kind:
                    work(kind, at, slice(0, 14) if kind == 4 else slice(None))
        give(kind)
    for copy in stores:
        copy.wait()


def make_outputs(norm, grads, firsts, seconds, anchors, outers, summed, groups):
    kinds = range(5)
    flat = tuple(v for kind in kinds for v in (firsts[kind], seconds[kind], anchors[kind], outers[kind], summed[kind]))
    flat += tuple(grads[:4])
    out = tuple(
        jax.ShapeDtypeStruct(shape, jnp.float32)
        for kind in kinds
        for shape in (firsts[kind].shape, firsts[kind].shape, anchors[kind].shape, anchors[kind].shape, firsts[kind].shape)
    )
    vm = pl.BlockSpec(memory_space=pltpu.VMEM)
    hbm = pl.BlockSpec(memory_space=pl.ANY)
    got = pl.pallas_call(
        functools.partial(outputs_kernel, anchors[0].shape[0], groups),
        out_shape=out,
        in_specs=[vm] * 2 + [hbm] * 29,
        out_specs=[hbm] * 25,
        scratch_shapes=[pltpu.VMEM(v.shape, jnp.float32) for v in flat]
        + [pltpu.VMEM(v.shape, jnp.float32) for v in out]
        + [pltpu.SemaphoreType.DMA((29,)), pltpu.SemaphoreType.DMA((25,))],
        compiler_params=pltpu.CompilerParams(vmem_limit_bytes=VMEM_LIMIT),
        name="make_outputs",
    )(norm, grads[4], *flat)
    return [[got[kind * 5 + j] for kind in kinds] for j in range(5)]


def class_forward(rows, mixed, place, attn_w, ffn_w, vec):
    width = rows.shape[1]
    h_embed = layer_norm(rows.astype(jnp.float32) + place[:1], vec[0], vec[1])
    x_attn = h_embed + (dot(mixed, low16(attn_w[:, 3 * width :])) + vec[4])
    h_attn = layer_norm(x_attn, vec[5], vec[6])
    h_low = low16(h_attn)
    pre = dot(h_low, low16(ffn_w[0])) + vec[10:].reshape(-1)
    act = low16(gelu_tanh(pre))
    x_ffn = h_attn + (dot_last(act, low16(ffn_w[1])) + vec[7])
    h_out = layer_norm(x_ffn, vec[8], vec[9])
    return low16(h_out), (x_attn, h_low, pre, act, x_ffn)


def class_backward(kept, mixed, attn_w, ffn_w, vec, d_cls):
    x_attn, h_low, pre, act, x_ffn = kept
    width = x_attn.shape[1]
    unused, out_back = jax.vjp(layer_norm, x_ffn, vec[8], vec[9])
    d_x_ffn, d_gain_two, d_shift_two = out_back(d_cls)
    d_branch = low16(d_x_ffn)
    d_down_bias = jnp.sum(d_branch, 0, dtype=jnp.float32)
    d_down = dot_rows(d_branch, act)
    d_act = dot(d_branch, low16(ffn_w[1]))
    unused, gelu_back = jax.vjp(gelu_tanh, pre)
    d_pre = low16(gelu_back(d_act)[0])
    d_up_bias = jnp.sum(d_pre, 0, dtype=jnp.float32)
    d_up = dot_rows(h_low, d_pre)
    d_h_attn = d_x_ffn + dot_last(d_pre, low16(ffn_w[0]))
    unused, attn_back = jax.vjp(layer_norm, x_attn, vec[5], vec[6])
    d_x_attn, d_gain_one, d_shift_one = attn_back(d_h_attn)
    d_proj = low16(d_x_attn)
    d_out_bias = jnp.sum(d_proj, 0, dtype=jnp.float32)
    d_w_out = dot_rows(mixed, d_proj)
    d_mixed = low16(dot_last(d_proj, low16(attn_w[:, 3 * width :])))
    rows = (d_out_bias, d_gain_one, d_shift_one, d_down_bias, d_gain_two, d_shift_two)
    return d_mixed, d_x_attn, d_w_out, jnp.stack([d_up, d_down]), rows, d_up_bias


def softmax_terms(scores, drop, target, weight, count, axis):
    masked = jnp.where(drop, MASKED, scores)
    top = jnp.max(masked, axis, keepdims=True)
    expo = jnp.exp(masked - top)
    total = jnp.sum(expo, axis, keepdims=True)
    lse = top + jnp.log(total)
    picked = jnp.sum(jnp.where(target, scores, 0.0), axis, keepdims=True)
    loss = jnp.sum(weight * (lse - picked))
    grad = low16((weight / count) * (expo / total - target.astype(jnp.float32)))
    return grad, loss


def score_stage(every_q, every_p, keys_q, keys_p, valid_q):
    count = jnp.maximum(jnp.sum(valid_q).astype(jnp.float32), 1.0)
    scale = every_q.shape[1] ** (-0.5)
    index_q = jnp.arange(every_q.shape[0])[:, None]
    index_p = jnp.arange(every_p.shape[0])[None, :]
    scores = dot_last(every_q, every_p) * scale
    same = keys_q[:, None] == keys_p[None, :]
    target_qp = index_p == 2 * index_q
    valid = valid_q.astype(jnp.float32)[:, None]
    grad_qp, loss_qp = softmax_terms(scores, same & ~target_qp, target_qp, valid, count, 1)
    target_pq = index_p // 2 == index_q
    drop_pq = (same | (valid_q[:, None] == 0)) & ~target_pq
    owner_valid = jnp.repeat(valid_q, 2)
    weight_p = jnp.where(index_p[0] % 2 == 0, owner_valid, 0).astype(jnp.float32)[None, :]
    grad_pq, loss_pq = softmax_terms(scores, drop_pq, target_pq, weight_p, count, 0)
    d_q = (dot(grad_qp, every_p) + dot(grad_pq, every_p)) * scale
    d_p = (dot_rows(grad_pq, every_q) + dot_rows(grad_qp, every_q)) * scale
    return d_q, d_p, loss_qp + loss_pq, count


def body(
    question_ids,
    passage_ids,
    question_lengths,
    passage_lengths,
    question_keys,
    passage_keys,
    question_valid,
    word_table,
    positions,
    attention,
    feedforward,
    vectors,
    word_first,
    positions_first,
    attention_first,
    feedforward_first,
    vectors_first,
    word_second,
    positions_second,
    attention_second,
    feedforward_second,
    vectors_second,
    word_anchor,
    positions_anchor,
    attention_anchor,
    feedforward_anchor,
    vectors_anchor,
    word_outer,
    positions_outer,
    attention_outer,
    feedforward_outer,
    vectors_outer,
):
    width = word_table.shape[2]
    many = lax.axis_size("dp")
    count_q, seq_q = question_ids.shape
    count_p, seq_p = passage_ids.shape
    counts = (count_q, count_p)
    table = word_table[0]
    sizes = Sizes(many, count_q, count_p, table.shape[0])
    ids_q = jnp.where(jnp.arange(seq_q)[None, :] < question_lengths[:, None], question_ids, -1)
    ids_p = jnp.where(jnp.arange(seq_p)[None, :] < passage_lengths[:, None], passage_ids, -1)
    half = count_q // 2
    flags = jnp.concatenate([question_keys, question_valid, passage_keys])
    flags = jnp.pad(flags, (0, 8 * 128 - flags.size)).reshape(8, 128)
    raw = jnp.concatenate(
        [
            ids_p[:, :128],
            ids_p[:, 128:],
            jnp.concatenate([ids_q[:half], ids_q[half:]], 1),
            flags,
        ]
    ).astype(jnp.int16)
    every, class_rows = exchange_rows(many, count_q, count_p, raw, table)
    flags_all = every[:, RAW_FLAGS, :].astype(jnp.int32)
    keys_q = flags_all[:, :count_q].reshape(-1)
    valid_all = flags_all[:, count_q : 2 * count_q].reshape(-1)
    keys_p = flags_all[:, 2 * count_q : 2 * count_q + count_p].reshape(-1)
    part, lse_part, query, kept, entry, levels = tokens_forward(
        sizes, every, class_rows, table, positions, attention, vectors
    )
    mixed_all, lse_all = exchange_mixed(sizes, part, lse_part)
    cuts = ((0, count_q), (count_q, count_q + count_p))
    cls, class_kept, mixes, class_x = ([], [], [], [])
    for enc in range(2):
        low, high = cuts[enc]
        rows = class_rows[:, low:high].reshape(-1, width)
        mixed = mixed_all[:, low:high].reshape(-1, width)
        low_cls, kept_cls = class_forward(
            rows, mixed, positions[0, enc], attention[0, enc], feedforward[0, enc], vectors[0, enc]
        )
        cls.append(low_cls)
        class_kept.append(kept_cls)
        mixes.append(mixed)
        class_x.append(rows.astype(jnp.float32) + positions[0, enc, :1])
    d_q, d_p, loss_total, count = score_stage(cls[0], cls[1], keys_q, keys_p, valid_all)
    d_cls = (d_q, d_p)
    finals, grad_parts, firsts_x = ([], [], [])
    for enc in range(2):
        d_mixed, d_x_attn, d_w_out, d_ffn, rows_mid, d_up_bias = class_backward(
            class_kept[enc], mixes[enc], attention[0, enc], feedforward[0, enc], vectors[0, enc], d_cls[enc]
        )
        grad_parts.append(d_mixed.reshape(many, counts[enc], width))
        firsts_x.append(d_x_attn)
        finals.append((d_w_out, d_ffn, rows_mid, d_up_bias))
    grad_all = jnp.concatenate(grad_parts, 1)
    d_query, d_table_t, slices, d_first = tokens_backward(
        sizes, levels, every, query, mixed_all, lse_all, grad_all, kept, entry, table, positions, attention, vectors
    )
    d_out = jnp.stack([finals[0][0], finals[1][0]])
    d_ffn = jnp.stack([finals[0][1], finals[1][1]])
    d_mid = jnp.stack(
        [
            jnp.concatenate(
                [
                    jnp.zeros((4, width), jnp.float32),
                    jnp.stack(list(part[2])),
                    part[3].reshape(-1, width),
                    jnp.zeros((2, width), jnp.float32),
                ]
            )
            for part in finals
        ]
    )
    weights = (word_table, positions, attention, feedforward, vectors)
    firsts = (word_first, positions_first, attention_first, feedforward_first, vectors_first)
    seconds = (word_second, positions_second, attention_second, feedforward_second, vectors_second)
    anchors = (word_anchor, positions_anchor, attention_anchor, feedforward_anchor, vectors_anchor)
    outers = (word_outer, positions_outer, attention_outer, feedforward_outer, vectors_outer)
    done = finish(
        sizes,
        d_query,
        slices.reshape(many, sizes.lines, 128),
        d_first,
        d_table_t,
        class_rows,
        every,
        firsts_x[0],
        firsts_x[1],
        d_out,
        d_ffn,
        d_mid,
        (positions, attention, vectors),
        (weights, firsts, seconds, anchors),
    )
    norm = done[0]
    grads = (done[1], done[2], done[3], d_ffn, done[4])
    first_new, second_new, averages, outer_next, weight_next = make_outputs(
        norm, grads, firsts, seconds, anchors, outers, done[5:10], lax.axis_size("grp")
    )
    norm = norm[0, 0]
    return (
        loss_total.reshape(1),
        count.reshape(1),
        norm.reshape(1),
        first_new[0],
        first_new[1],
        first_new[2],
        first_new[3],
        first_new[4],
        second_new[0],
        second_new[1],
        second_new[2],
        second_new[3],
        second_new[4],
        averages[0],
        averages[1],
        averages[2],
        averages[3],
        averages[4],
        outer_next[0],
        outer_next[1],
        outer_next[2],
        outer_next[3],
        outer_next[4],
        weight_next[0],
        weight_next[1],
        weight_next[2],
        weight_next[3],
        weight_next[4],
    )


def solution(mesh):
    placed = (
        P(("grp", "dp"), None),
        P(("grp", "dp"), None),
        P(("grp", "dp")),
        P(("grp", "dp")),
        P(("grp", "dp")),
        P(("grp", "dp")),
        P(("grp", "dp")),
        P("grp", "dp", None),
        P("grp", None, None, None),
        P("grp", None, None, None),
        P("grp", None, None, None, None),
        P("grp", None, None, None),
        P("grp", "dp", None),
        P("grp", None, None, None),
        P("grp", None, None, None),
        P("grp", None, None, None, None),
        P("grp", None, None, None),
        P("grp", "dp", None),
        P("grp", None, None, None),
        P("grp", None, None, None),
        P("grp", None, None, None, None),
        P("grp", None, None, None),
        P("dp", None),
        P(),
        P(),
        P(),
        P(),
        P("dp", None),
        P(),
        P(),
        P(),
        P(),
    )
    return jax.shard_map(
        body,
        mesh=mesh,
        in_specs=placed,
        out_specs=(
            P("grp"),
            P("grp"),
            P("grp"),
            P("grp", "dp", None),
            P("grp", None, None, None),
            P("grp", None, None, None),
            P("grp", None, None, None, None),
            P("grp", None, None, None),
            P("grp", "dp", None),
            P("grp", None, None, None),
            P("grp", None, None, None),
            P("grp", None, None, None, None),
            P("grp", None, None, None),
            P("dp", None),
            P(),
            P(),
            P(),
            P(),
            P("dp", None),
            P(),
            P(),
            P(),
            P(),
            P("grp", "dp", None),
            P("grp", None, None, None),
            P("grp", None, None, None),
            P("grp", None, None, None, None),
            P("grp", None, None, None),
        ),
        check_vma=False,
    )
```

profile of v0, /device:TPU:0, one launch (start us, length us, event | category | flops | bytes accessed | tf_op | source)
XLA Modules:
  0.0 269.0 jit_solution(5754135970657762500)
XLA Ops:
  0.7 0.7 convert.45
  2.8 0.7 slice_bitcast_fusion.22
  3.5 1.3 broadcast_multiply_fusion.7
  4.8 0.8 select_convert_fusion.1
  5.6 0.8 fusion.68
  6.4 0.8 slice_bitcast_fusion.15
  7.2 1.3 copy.80.vec_ref.refs_13_.refs_30_
  8.6 1.3 copy.88.refs_31_.refs_22_
  9.9 1.3 copy.89.refs_32_.refs_23_
  11.2 1.3 copy.90.refs_33_.refs_24_
  12.5 0.8 select_convert_fusion
  13.3 0.7 pad_add_fusion.raw_ref
  14.0 1.3 copy.94.refs_25_
  15.5 1.1 convert.48
  16.6 35.9 %exchange_rows.1 = (s16[16,80,128]{2,1,0:T(8,128)(2,1)}, bf16[16,48,128]{2,1,0:T(8,128)(2,1)}) custom-call(s16[80,128]{1,0:T(8,128)(2,1)} %pad_add_fusion.raw_ref, f32[1920,128]{1,0:T(8,128)} %bitcast.157), custom_call_target="tpu_custom_call" | custom-call | tf_op jit(solution)/shard_map/exchange_rows/pallas_call | solution.py:186
  52.5 0.8 slice_convert_fusion
  53.5 1.0 add_reduce_fusion.1
  54.5 1.0 multiply_reduce_fusion.14
  55.6 1.1 add_reduce_fusion
  56.8 1.2 multiply_reduce_fusion.6
  58.0 0.7 slice_reduce_fusion
  60.1 1.0 fusion.33
  61.4 1.1 fusion.28
  62.6 55.0 %tokens_forward.1 = (bf16[16,48,128]{2,1,0:T(8,128)(2,1)}, f32[16,8,128]{2,1,0:T(8,128)}, bf16[16,48,128]{2,1,0:T(8,128)(2,1)}, f32[18,136,512]{2,1,0:T(8,128)}, s32[18,8,512]{2,1,0:T(8,128)}, /*index=5*/s32[1]{0:T(128)}) custom-call(s16[16,80,128]{2,1,0:T(8,128)(2,1)} %get-tuple-element.77.raw_ref.refs_5_, ...), custom_call_target="tpu_custom_call" | custom-call | tf_op jit(solution)/shard_map/tokens_forward/pallas_call | solution.py:499
  117.6 17.6 %exchange_mixed.1 = (bf16[16,48,128]{2,1,0:T(8,128)(2,1)}, f32[16,8,128]{2,1,0:T(8,128)}) custom-call(bf16[16,48,128]{2,1,0:T(8,128)(2,1)} %get-tuple-element.79.part_ref, f32[16,8,128]{2,1,0:T(8,128)} %get-tuple-element.80.lse_ref), custom_call_target="tpu_custom_call" | custom-call | tf_op jit(solution)/shard_map/exchange_mixed/pallas_call | solution.py:580
  135.2 0.9 slice.217
  136.5 0.9 slice.233
  142.4 1.3 multiply_convert_fusion.2
  143.8 0.7 multiply_reduce_fusion.16
  146.0 1.5 multiply_reduce_fusion.8
  147.5 1.0 fusion.74
  148.5 1.2 multiply_reduce_fusion
  149.7 1.0 fusion.66
  150.8 0.9 fusion.64
  152.0 1.2 convolution_bitcast_fusion
  153.2 0.8 convert_reduce_fusion
  158.7 0.7 pad_maximum_fusion.1.grad_ref
  159.3 37.8 %tokens_backward.1 = (bf16[16,48,128]{2,1,0:T(8,128)(2,1)}, f32[128,2048]{1,0:T(8,128)}, bf16[2,4,128,128]{3,2,1,0:T(8,128)(2,1)}, f32[8,128]{1,0:T(8,128)}) custom-call(s32[1]{0:T(128)} %get-tuple-element.82.levels_ref, s16[16,80,128]{2,1,0:T(8,128)(2,1)} %get-tuple-element.77.raw_ref.refs_5_, bf16[16,48,128]{2,1,0:T(8,128)(2,1)} %get-tuple-element.83.query_ref, ...), custom_call_target="tpu_custom_call" | custom-call | tf_op jit(solution)/shard_map/tokens_backward/pallas_call | solution.py:499
  197.3 0.7 pad_maximum_fusion.2.refs_8_
  198.1 1.1 pad_maximum_fusion.refs_9_.refs_30_
  199.2 47.3 %finish.1 = (f32[8,128]{1,0:T(8,128)}, f32[1920,128]{1,0:T(8,128)}, f32[2,256,128]{2,1,0:T(8,128)}, f32[2,128,512]{2,1,0:T(8,128)}, f32[2,16,128]{2,1,0:T(8,128)...) custom-call(bf16[16,48,128]{2,1,0:T(8,128)(2,1)} %get-tuple-element., ...), custom_call_target="tpu_custom_call" | custom-call | tf_op jit(solution)/shard_map/finish/pallas_call | solution.py:1001
  246.5 1.2 slice.245
  247.7 12.4 %make_outputs.1 = (f32[1,1920,128]{2,1,0:T(8,128)}, f32[1,1920,128]{2,1,0:T(8,128)}, f32[1920,128]{1,0:T(8,128)}, f32[1920,128]{1,0:T(8,128)}, f32[1,1920,128]{2...) custom-call(f32[8,128]{1,0:T(8,128)} %get-tuple-element.91.refs_0_, ...), custom_call_target="tpu_custom_call" | custom-call | tf_op jit(solution)/shard_map/make_outputs/pallas_call | solution.py:1105
  260.2 1.3 copy.95
  261.5 1.3 copy.96
  262.8 1.3 copy.97
  264.1 1.3 copy.98
  265.5 1.3 copy.99
  (113 shorter events, 13.9 us)
Async XLA Ops:
  0.7 61.8 %copy-start.1 = (f32[1,2,2,128,512]{4,3,2,1,0:T(8,128)S(1)}, f32[1,2,2,128,512]{4,3,2,1,0:T(8,128)}, u32[]{:S(2)}) copy-start(f32[1,2,2,128,512]{4,3,2,1,0:T(8,128)} %refs_26_.1) | copy-start | bytes 3145732
  2.8 138.3 %copy-start.10 = (s32[256]{0:T(256)}, s32[256]{0:T(256)S(1)}, u32[]{:S(2)}) copy-start(s32[256]{0:T(256)S(1)} %iota_multiply_fusion) | copy-start | bytes 3076
  7.2 131.0 %copy-start.6 = (f32[128]{0:T(128)}, f32[128]{0:T(128)S(1)}, u32[]{:S(2)}) copy-start(f32[128]{0:T(128)S(1)} %get-tuple-element.236) | copy-start | bytes 1540
  7.2 133.9 %copy-start.8 = (f32[128]{0:T(128)}, f32[128]{0:T(128)S(1)}, u32[]{:S(2)}) copy-start(f32[128]{0:T(128)S(1)} %get-tuple-element.233) | copy-start | bytes 1540
  7.2 135.2 %copy-start.9 = (f32[128]{0:T(128)}, f32[128]{0:T(128)S(1)}, u32[]{:S(2)}) copy-start(f32[128]{0:T(128)S(1)} %get-tuple-element.234) | copy-start | bytes 1540
  59.6 81.5 %copy-start.12 = (pred[256]{0:T(512)(128)(4,1)}, pred[256]{0:T(512)(128)(4,1)S(1)}, u32[]{:S(2)}) copy-start(pred[256]{0:T(512)(128)(4,1)S(1)} %broadcast_compare_fusion) | copy-start | bytes 772
  138.3 0.8 copy-start.3
  138.3 4.1 %copy-start.11 = (f32[256]{0:T(256)S(1)}, f32[256]{0:T(256)}, u32[]{:S(2)}) copy-start(f32[256]{0:T(256)} %convert_divide_fusion.1) | copy-start | bytes 3076
  153.2 2.7 %copy-start.4 = (f32[256,512]{1,0:T(8,128)S(1)}, f32[256,512]{1,0:T(8,128)}, u32[]{:S(2)}) copy-start(f32[256,512]{1,0:T(8,128)} %copy-done.3) | copy-start | bytes 1572868
  154.4 2.9 %copy-start.7 = (f32[128]{0:T(128)S(1)}, f32[128]{0:T(128)}, u32[]{:S(2)}) copy-start(f32[128]{0:T(128)} %copy-done.6) | copy-start | bytes 1540
  154.8 3.1 %copy-start.13 = (f32[128]{0:T(128)S(1)}, f32[128]{0:T(128)}, u32[]{:S(2)}) copy-start(f32[128]{0:T(128)} %get-tuple-element.192) | copy-start | bytes 1540
  154.9 3.1 %copy-start.14 = (f32[128]{0:T(128)S(1)}, f32[128]{0:T(128)}, u32[]{:S(2)}) copy-start(f32[128]{0:T(128)} %get-tuple-element.198) | copy-start | bytes 1540
  155.4 41.7 %copy-start = (f32[512,128]{1,0:T(8,128)}, f32[512,128]{1,0:T(8,128)S(1)}, u32[]{:S(2)}) copy-start(f32[512,128]{1,0:T(8,128)S(1)} %get-tuple-element.207.refs_7_) | copy-start | bytes 786436
  157.3 40.7 %copy-start.5 = (f32[1,128,512]{2,1,0:T(8,128)S(1)}, f32[1,128,512]{2,1,0:T(8,128)}, u32[]{:S(2)}) copy-start(f32[1,128,512]{2,1,0:T(8,128)} %convolution_bitcast_fusion) | copy-start | bytes 786436
  157.8 40.3 %copy-start.2 = (f32[256,128]{1,0:T(8,128)}, f32[256,128]{1,0:T(8,128)S(1)}, u32[]{:S(2)}) copy-start(f32[256,128]{1,0:T(8,128)S(1)} %get-tuple-element.203.refs_6_) | copy-start | bytes 393220
where the time goes:
time: 271 us; the launch traced here: 269 us
  Pallas kernels  206 us (76%)
  other arithmetic  25.9 us (10%)
  local copies, waits for them, and re-layouts  20 us (7%)
  matrix products  11.7 us (4%)
  between operations  5.42 us (2%)
    pallas_call x2, Pallas kernels, local_call(): pl.pallas_call(kernel, out_shape=out_shape, in_specs=[sm if i in smem_in...  92.8 us
    pallas_call x1, Pallas kernels, finish(): pl.pallas_call(functools.partial(finish_kernel, sizes), out_shape=tuple((...  47.3 us
    pallas_call x1, Pallas kernels, exchange_rows(): pl.pallas_call(functools.partial(rows_kernel, many, count_q), out_shape=(...  35.9 us
    pallas_call x1, Pallas kernels, remote_call(): pl.pallas_call(kernel, out_shape=out_shape, in_specs=[pl.BlockSpec(memory...  17.6 us
    unnamed x40, local copies, waits for them, and re-layouts  13.5 us
    pallas_call x1, Pallas kernels, make_outputs(): pl.pallas_call(functools.partial(outputs_kernel, anchors[0].shape[0], gro...  12.4 us

commit v1 on v0

--- a/solution.py
+++ b/solution.py
@@ -47,6 +47,7 @@
 SLOTS = 128
 SPAN = WAYS * SLOTS
 CHUNK = 256
+UNROLL = 2
 RAW_Q = 64
 RAW_FLAGS = 72
 RAW_ROWS = 80
@@ -132,42 +133,82 @@
 
 
 def rows_kernel(
-    many, count_q, raw_ref, table_ref, every_ref, rows_ref, low_ref, offer, landed, own, send, recv
+    many,
+    question_ref,
+    passage_ref,
+    length_q,
+    length_p,
+    key_q,
+    valid_q,
+    key_p,
+    table_ref,
+    every_ref,
+    rows_ref,
+    stage,
+    raw,
+    low_ref,
+    offer,
+    landed,
+    own,
+    send,
+    recv,
 ):
+    count_q, count_p = (question_ref.shape[0], passage_ref.shape[0])
+    half = count_q // 2
+    lane = iota((1, 128), 1)
+    for seq in range(count_p):
+        stop = length_p[seq]
+        stage[seq : seq + 1, :] = jnp.where(lane < stop, passage_ref[seq : seq + 1, 0:128], -1)
+        stage[count_p + seq : count_p + seq + 1, :] = jnp.where(
+            lane + 128 < stop, passage_ref[seq : seq + 1, 128:256], -1
+        )
+    both = jnp.concatenate([question_ref[0:half, :], question_ref[half:count_q, :]], 1)
+    for seq in range(half):
+        stop = jnp.where(lane < 64, length_q[seq], length_q[half + seq] + 64)
+        stage[RAW_Q + seq : RAW_Q + seq + 1, :] = jnp.where(lane < stop, both[seq : seq + 1], -1)
+    flags = jnp.zeros((1, 128), jnp.int32)
+    for spot in range(count_q):
+        flags = jnp.where(lane == spot, key_q[spot], flags)
+        flags = jnp.where(lane == count_q + spot, valid_q[spot], flags)
+    for spot in range(count_p):
+        flags = jnp.where(lane == 2 * count_q + spot, key_p[spot], flags)
+    stage[RAW_FLAGS:RAW_ROWS, :] = jnp.broadcast_to(flags, (8, 128))
+    raw[...] = stage[...].astype(jnp.int16)
     me = enter(many)
-    raw_pairs = [(lambda peer: raw_ref, every_ref)]
+    raw_pairs = [(lambda peer: raw, every_ref)]
     spread_start(many, me, raw_pairs, send, recv, 0)
-    every_ref[me] = raw_ref[...]
+    every_ref[me] = raw[...]
     depth = table_ref.shape[0]
     low_ref[...] = jnp.zeros_like(low_ref)
     low_ref[0:depth, :] = low16(table_ref[...])
     padded = low_ref.shape[0]
     spread_wait(many, me, raw_pairs, send, recv, 0)
     first = me * depth
+    block = math.gcd(many, 16)
 
     def pick(step, carry):
-        peer = lax.rem(me + step, many)
-        found = every_ref[peer].astype(jnp.int32)
-        ask = jnp.concatenate(
-            [
-                found[RAW_Q : RAW_Q + count_q // 2, 0:1],
-                found[RAW_Q : RAW_Q + count_q // 2, 64:65],
-                found[0 : RAW_Q // 2, 0:1],
-            ],
-            0,
-        )
-        place = ask - first
-        inside = (place >= 0) & (place < depth)
-        spot = jnp.where(inside, place, -1)
-        total = jnp.zeros((spot.shape[0], 128), jnp.float32)
-        for cut in range(padded // CHUNK):
-            wide = jnp.broadcast_to(spot, (spot.shape[0], CHUNK))
-            chosen = hot(wide == iota(wide.shape, 1) + cut * CHUNK)
-            total += dot(chosen, low_ref[cut * CHUNK : (cut + 1) * CHUNK, :])
-        offer[peer] = low16(total)
+        asks = []
+        for i in range(block):
+            found = every_ref[step * block + i].astype(jnp.int32)
+            asks += [
+                found[RAW_Q : RAW_Q + half, 0:1],
+                found[RAW_Q : RAW_Q + half, 64:65],
+                found[0:count_p, 0:1],
+            ]
+        place = jnp.concatenate(asks, 0) - first
+        spot = jnp.where((place >= 0) & (place < depth), place, -1)
+        number = spot.shape[0]
+        total = jnp.zeros((number, 128), jnp.float32)
+        wide = jnp.broadcast_to(spot, (number, CHUNK))
+        for at in range(padded // CHUNK):
+            chosen = hot(wide == iota((number, CHUNK), 1) + at * CHUNK)
+            total += dot(chosen, low_ref[at * CHUNK : (at + 1) * CHUNK, :])
+        each = count_q + count_p
+        for i in range(block):
+            offer[step * block + i] = low16(total[i * each : (i + 1) * each])
         return carry
 
-    lax.fori_loop(0, many, pick, 0)
+    lax.fori_loop(0, many // block, pick, 0)
     pairs = [(lambda peer: offer.at[peer], landed)]
     spread_start(many, me, pairs, send, recv, 1)
     landed[me] = offer[me]
@@ -179,19 +220,24 @@
     spread_wait(many, me, pairs, send, recv, 2)
 
 
-def exchange_rows(many, count_q, count_p, raw, table):
+def exchange_rows(many, ids_q, ids_p, length_q, length_p, key_q, valid_q, key_p, table):
+    count_q, count_p = (ids_q.shape[0], ids_p.shape[0])
     depth = table.shape[0]
     padded = -(-depth // CHUNK) * CHUNK
     both = count_q + count_p
+    vm = pl.BlockSpec(memory_space=pltpu.VMEM)
+    sm = pl.BlockSpec(memory_space=pltpu.SMEM)
     return pl.pallas_call(
-        functools.partial(rows_kernel, many, count_q),
+        functools.partial(rows_kernel, many),
         out_shape=(
             jax.ShapeDtypeStruct((many, RAW_ROWS, 128), jnp.int16),
             jax.ShapeDtypeStruct((many, both, 128), jnp.bfloat16),
         ),
-        in_specs=[pl.BlockSpec(memory_space=pltpu.VMEM)] * 2,
-        out_specs=[pl.BlockSpec(memory_space=pltpu.VMEM)] * 2,
+        in_specs=[vm, vm, sm, sm, sm, sm, sm, vm],
+        out_specs=[vm, vm],
         scratch_shapes=[
+            pltpu.VMEM((RAW_ROWS, 128), jnp.int32),
+            pltpu.VMEM((RAW_ROWS, 128), jnp.int16),
             pltpu.VMEM((padded, 128), jnp.bfloat16),
             pltpu.VMEM((many, both, 128), jnp.bfloat16),
             pltpu.VMEM((many, both, 128), jnp.bfloat16),
@@ -203,7 +249,7 @@
             collective_id=1, has_side_effects=True, vmem_limit_bytes=VMEM_LIMIT
         ),
         name="exchange_rows",
-    )(raw, table)
+    )(ids_q, ids_p, length_q, length_p, key_q, valid_q, key_p, table)
 
 
 def norm_rows(values, gain, shift):
@@ -240,9 +286,14 @@
         self.keep = self.spans * 136 * SPAN * 4 <= 8 * 1024 * 1024
 
 
-def prepare_tokens(sizes, table_ref, place_ref, attn_ref, vec_ref, table_t, place_t, w_kv, vec_t):
-    table_t[...] = jnp.zeros_like(table_t)
+def vector_row(vec_ref, enc, row):
+    return vec_ref[0, row, enc : enc + 1, :]
+
+
+def prepare_tokens(sizes, table_ref, place_ref, table_t, place_t):
     depth = sizes.depth
+    if sizes.padded > depth:
+        table_t[...] = jnp.zeros_like(table_t)
     for cut in range(0, depth, 128):
         top = min(cut + 128, depth)
         piece = table_ref[cut:top, :]
@@ -264,9 +315,8 @@
             w_kv[enc, cut * 128 : (cut + 1) * 128, :] = low16(
                 jnp.transpose(attn_ref[0, enc, :, (cut + 1) * 128 : (cut + 2) * 128])
             )
-        rows = jnp.concatenate(
-            [vec_ref[0, enc, 0:10, :], jnp.zeros((118, 128), jnp.float32)], 0
-        )
+        rows = [vector_row(vec_ref, enc, row) for row in range(4)]
+        rows = jnp.concatenate(rows + [jnp.zeros((124, 128), jnp.float32)], 0)
         vec_t[enc] = jnp.transpose(rows)
 
 
@@ -274,7 +324,7 @@
     return jnp.take_along_axis(values, lanes, axis=1, mode="promise_in_bounds")
 
 
-def pack_span(sizes, enc, step, level, first, raw_ref, entries, counts):
+def pack_span(sizes, enc, step, level, first, raw_ref):
     if enc == 1:
         ids = raw_ref[step, 0:RAW_Q, :].astype(jnp.int32)
     else:
@@ -288,15 +338,14 @@
     place = ids - first
     owned = (place >= 0) & (place < sizes.depth)
     flag = hot(owned)
-    tall = iota((64, 64), 0)
     inside = dot(flag, hot(iota((128, 128), 0) <= iota((128, 128), 1)))
     total = dot(flag, jnp.ones((128, 128), jnp.bfloat16))
-    before = dot(hot(iota((64, 64), 1) < tall), low16(total))
-    counts[...] = jnp.maximum(counts[...], (before + total)[56:64])
+    before = dot(hot(iota((64, 64), 1) < iota((64, 64), 0)), low16(total))
     reached = (inside + before).astype(jnp.int32)
     start = before.astype(jnp.int32)
     stop = (before + total).astype(jnp.int32)
     line = iota((64, 128), 0)
+    codes = []
     for window in range(WAYS):
         slot = iota((64, 128), 1) + (window * SLOTS + level * SPAN)
         lane = jnp.zeros((64, 128), jnp.int32)
@@ -312,12 +361,11 @@
             seq = (line >> 3) * sizes.count[0] + (lane >> 6) * 8 + (line & 7) + 1
         code = (row << 16) + (where << 8) + seq
         code = jnp.where((slot >= start) & (slot < stop), code, 0)
-        entries[0:1, window * SLOTS : (window + 1) * SLOTS] = jnp.sum(code, 0, keepdims=True)
-
-
-def gather_span(sizes, enc, step, level, first, raw_ref, table_t, place_t, entries, counts, scaled_ref):
-    pack_span(sizes, enc, step, level, first, raw_ref, entries, counts)
-    code = entries[0:1, :]
+        codes.append(jnp.sum(code, 0, keepdims=True))
+    return jnp.concatenate(codes, 1), (before + total)[56:64]
+
+
+def gather_span(sizes, enc, code, table_t, place_t):
     rows = code >> 16
     where = (code >> 8) & 255
     x = jnp.zeros((128, SPAN), jnp.float32)
@@ -329,8 +377,7 @@
     x += dot(place_t[enc, 0], chosen) + dot(place_t[enc, 1], chosen)
     center = x - jnp.mean(x, 0, keepdims=True)
     rate = lax.rsqrt(jnp.mean(center * center, 0, keepdims=True) + NORM_EPS)
-    scaled_ref[0:128, :] = center * rate
-    scaled_ref[128:129, :] = rate
+    return center * rate, rate
 
 
 def project(enc, scaled, vec_t, w_kv):
@@ -339,6 +386,12 @@
     keys_t = low16(kv[:128])
     values_t = low16(kv[128:] + vec_t[enc, :, 3:4])
     return a_t, keys_t, values_t
+
+
+def own_slots(code, number):
+    line = iota((2 * number, SPAN), 0)
+    line = jnp.where(line >= number, line - number, line)
+    return line == (code & 255) - 1
 
 
 def forward_kernel(
@@ -359,9 +412,6 @@
     place_t,
     w_kv,
     vec_t,
-    entries,
-    counts,
-    scaled_ref,
     query_q,
     total_q,
     top_q,
@@ -372,113 +422,117 @@
 ):
     first = lax.axis_index("dp") * sizes.depth
     count_q, count_p = sizes.count
-    prepare_tokens(sizes, table_ref, place_ref, attn_ref, vec_ref, table_t, place_t, w_kv, vec_t)
+    prepare_tokens(sizes, table_ref, place_ref, table_t, place_t)
     prepare_weights(attn_ref, vec_ref, w_kv, vec_t)
-    counts[...] = jnp.zeros_like(counts)
+    block = math.gcd(sizes.many, 16)
     for enc in range(2):
         low, high = (0, count_q) if enc == 0 else (count_q, count_q + count_p)
         w_q = low16(attn_ref[0, enc, :, 0:128])
 
         def ask(step, carry):
+            spot = pl.ds(step * block, block)
+            held = rows_ref[spot, low:high, :].reshape(block * (high - low), 128)
+            x = held.astype(jnp.float32) + place_ref[0, enc, 0:1, :]
+            h = norm_rows(x, vector_row(vec_ref, enc, 0), vector_row(vec_ref, enc, 1))
+            query = low16(dot(low16(h), w_q) + vector_row(vec_ref, enc, 2))
+            query_ref[spot, low:high, :] = query.reshape(block, high - low, 128)
             if enc == 0:
-                held = jnp.concatenate(
-                    [rows_ref[step * 8 + i, low:high, :] for i in range(8)], 0
-                )
-            else:
-                held = rows_ref[step, low:high, :]
-            x = held.astype(jnp.float32) + place_ref[0, enc, 0:1, :]
-            h = norm_rows(x, vec_ref[0, enc, 0:1, :], vec_ref[0, enc, 1:2, :])
-            query = low16(dot(low16(h), w_q) + vec_ref[0, enc, 2:3, :])
-            if enc == 0:
-                query_q[step] = query
-                for i in range(8):
-                    query_ref[step * 8 + i, low:high, :] = query[i * count_q : (i + 1) * count_q]
-            else:
-                query_ref[step, low:high, :] = query
+                for half in range(block // 8):
+                    query_q[step * (block // 8) + half] = query[half * 8 * count_q : (half + 1) * 8 * count_q]
             return carry
 
-        lax.fori_loop(0, sizes.steps[enc], ask, 0)
-    total_q[...] = jnp.zeros_like(total_q)
-    total_p[...] = jnp.zeros_like(total_p)
-    mass_q[...] = jnp.zeros_like(mass_q)
-    mass_p[...] = jnp.zeros_like(mass_p)
-    top_q[...] = jnp.full_like(top_q, NEG)
-    top_p[...] = jnp.full_like(top_p, NEG)
+        lax.fori_loop(0, sizes.many // block, ask, 0)
+    states = ((total_q, top_q, mass_q), (total_p, top_p, mass_p))
+    for total, top, mass in states:
+        total[...] = jnp.zeros_like(total)
+        mass[...] = jnp.zeros_like(mass)
+        top[...] = jnp.full_like(top, NEG)
 
     def one_level(state):
         level = state[0]
+        count = state[2]
         for enc in range(2):
-            total, top, mass = (total_q, top_q, mass_q) if enc == 0 else (total_p, top_p, mass_p)
-
-            def one_span(step, carry):
-                gather_span(
-                    sizes, enc, step, level, first, raw_ref, table_t, place_t, entries, counts, scaled_ref
-                )
-                scaled = scaled_ref[0:128, :]
-                if sizes.keep:
-                    at = step if enc == 0 else sizes.steps[0] + step
-
-                    @pl.when(level == 0)
-                    def _():
-                        kept_ref[at] = scaled_ref[...]
-                        entry_ref[at] = entries[...]
-
-                a_t, keys_t, values_t = project(enc, scaled, vec_t, w_kv)
-                query = query_q[step] if enc == 0 else query_ref[step, count_q:, :]
-                both = two_heads(query)
-                number = query.shape[0]
-                scores = dot(both, keys_t) * HEAD ** (-0.5)
-                seq = (entries[0:1, :] & 255) - 1
-                line = iota(scores.shape, 0)
-                line = jnp.where(line >= number, line - number, line)
-                mine = line == seq
-                scores = jnp.where(mine, scores, NEG)
-                old = top[step][:, 0:1]
-                new = jnp.maximum(old, jnp.max(scores, 1, keepdims=True))
-                fade = jnp.exp(old - new)
-                expo = jnp.where(mine, jnp.exp(scores - new), 0.0)
-                mass[step] = mass[step] * fade + jnp.sum(expo, 1, keepdims=True)
-                top[step] = jnp.broadcast_to(new, top.shape[1:])
-                mixed = dot_last(low16(expo), values_t)
-                total[step] = total[step] * fade + mixed
-                return carry
-
-            lax.fori_loop(0, sizes.steps[enc], one_span, 0)
-        need = (jnp.max(counts[...]).astype(jnp.int32) + SPAN - 1) // SPAN
-        return level + 1, jnp.maximum(need, 1)
-
-    last = lax.while_loop(lambda state: state[0] < state[1], one_level, (jnp.int32(0), jnp.int32(1)))
+            total, top, mass = states[enc]
+
+            def spans(turn, count):
+                steps = [turn * UNROLL + u for u in range(UNROLL)]
+                old = [(total[s], top[s][:, 0:1], mass[s]) for s in steps]
+                queries = [query_q[s] if enc == 0 else query_ref[s, count_q:, :] for s in steps]
+                packed = [pack_span(sizes, enc, s, level, first, raw_ref) for s in steps]
+                codes = [part[0] for part in packed]
+                for part in packed:
+                    count = jnp.maximum(count, part[1])
+                found = [gather_span(sizes, enc, code, table_t, place_t) for code in codes]
+                made = [project(enc, part[0], vec_t, w_kv) for part in found]
+                scores = [
+                    dot(two_heads(query), part[1]) * HEAD ** (-0.5) for query, part in zip(queries, made)
+                ]
+                news = []
+                for u in range(UNROLL):
+                    mine = own_slots(codes[u], queries[u].shape[0])
+                    score = jnp.where(mine, scores[u], NEG)
+                    new = jnp.maximum(old[u][1], jnp.max(score, 1, keepdims=True))
+                    fade = jnp.exp(old[u][1] - new)
+                    expo = jnp.where(mine, jnp.exp(score - new), 0.0)
+                    news.append(
+                        (
+                            old[u][0] * fade + dot_last(low16(expo), made[u][2]),
+                            jnp.broadcast_to(new, top.shape[1:]),
+                            old[u][2] * fade + jnp.sum(expo, 1, keepdims=True),
+                        )
+                    )
+                for u, s in enumerate(steps):
+                    total[s] = news[u][0]
+                    top[s] = news[u][1]
+                    mass[s] = news[u][2]
+                    if sizes.keep:
+                        at = s if enc == 0 else sizes.steps[0] + s
+                        at = jnp.where(level == 0, at, sizes.spans)
+                        kept_ref[at, 0:128, :] = found[u][0]
+                        kept_ref[at, 128:129, :] = found[u][1]
+                        entry_ref[at, 0:1, :] = codes[u]
+                return count
+
+            count = lax.fori_loop(0, sizes.steps[enc] // UNROLL, spans, count)
+        need = (jnp.max(count).astype(jnp.int32) + SPAN - 1) // SPAN
+        return level + 1, jnp.maximum(need, 1), count
+
+    last = lax.while_loop(
+        lambda state: state[0] < state[1],
+        one_level,
+        (jnp.int32(0), jnp.int32(1), jnp.zeros((8, 128), jnp.float32)),
+    )
     levels_ref[0] = last[1]
     lse_ref[...] = jnp.full_like(lse_ref, NEG)
     for enc in range(2):
-        total, top, mass = (total_q, top_q, mass_q) if enc == 0 else (total_p, top_p, mass_p)
-
-        def close(step, carry):
-            bulk = mass[step]
-            some = bulk > 0.0
-            safe = jnp.where(some, bulk, 1.0)
-            mixed = merge_heads(total[step] / safe)
-            lse = jnp.where(some, top[step] + jnp.log(safe), NEG)
-            if enc == 1:
-                out_ref[step, count_q:, :] = low16(mixed)
-                tall = jnp.concatenate([lse, jnp.full((128 - 2 * count_p, 128), NEG, jnp.float32)], 0)
-                lse_ref[step, 0:1, :] = jnp.transpose(tall)[0:1, :]
-            else:
-                half = lse.shape[0] // 2
-                for i in range(8):
-                    out_ref[step * 8 + i, 0:count_q, :] = low16(mixed[i * count_q : (i + 1) * count_q])
-                    tall = jnp.concatenate(
-                        [
-                            lse[i * count_q : (i + 1) * count_q],
-                            lse[half + i * count_q : half + (i + 1) * count_q],
-                            jnp.full((128 - 2 * count_q, 128), NEG, jnp.float32),
-                        ],
-                        0,
-                    )
-                    lse_ref[step * 8 + i, 1:2, :] = jnp.transpose(tall)[0:1, :]
+        total, top, mass = states[enc]
+
+        def close(turn, carry):
+            for u in range(UNROLL):
+                step = turn * UNROLL + u
+                bulk = mass[step]
+                some = bulk > 0.0
+                safe = jnp.where(some, bulk, 1.0)
+                mixed = merge_heads(total[step] / safe)
+                lse = jnp.where(some, top[step] + jnp.log(safe), NEG)
+                if enc == 1:
+                    out_ref[step, count_q:, :] = low16(mixed)
+                    at = iota(lse.shape, 0) == iota(lse.shape, 1)
+                    lse_ref[step, 0:1, :] = jnp.sum(jnp.where(at, lse, 0.0), 0, keepdims=True)
+                else:
+                    half = lse.shape[0] // 2
+                    row = iota((count_q, 128), 0)
+                    lane = iota((count_q, 128), 1)
+                    for i in range(8):
+                        spot = slice(i * count_q, (i + 1) * count_q)
+                        out_ref[step * 8 + i, 0:count_q, :] = low16(mixed[spot])
+                        line = jnp.where(lane == row, lse[spot], 0.0) + jnp.where(
+                            lane == row + count_q, lse[half + i * count_q : half + (i + 1) * count_q], 0.0
+                        )
+                        lse_ref[step * 8 + i, 1:2, :] = jnp.sum(line, 0, keepdims=True)
             return carry
 
-        lax.fori_loop(0, sizes.steps[enc], close, 0)
+        lax.fori_loop(0, sizes.steps[enc] // UNROLL, close, 0)
 
 
 def token_scratch(sizes):
@@ -487,9 +541,6 @@
         pltpu.VMEM((2, 2, 128, CHUNK), jnp.bfloat16),
         pltpu.VMEM((2, 256, 128), jnp.bfloat16),
         pltpu.VMEM((2, 128, 128), jnp.float32),
-        pltpu.VMEM((8, SPAN), jnp.int32),
-        pltpu.VMEM((8, 128), jnp.float32),
-        pltpu.VMEM((136, SPAN), jnp.float32),
     ]
 
 
@@ -510,7 +561,7 @@
 def tokens_forward(sizes, every, rows, table, positions, attention, vectors):
     many = sizes.many
     both = sum(sizes.count)
-    kept = sizes.spans if sizes.keep else 1
+    kept = sizes.spans + 1 if sizes.keep else 1
     state = []
     for enc in range(2):
         tall = 2 * sizes.queries[enc]
@@ -636,9 +687,6 @@
     place_t,
     w_kv,
     vec_t,
-    entries,
-    counts,
-    scaled_ref,
     d_place_ref,
     d_attn_ref,
     acc_gain,
@@ -650,121 +698,119 @@
     first = lax.axis_index("dp") * sizes.depth
     count_q, count_p = sizes.count
     prepare_weights(attn_ref, vec_ref, w_kv, vec_t)
-    again = levels_ref[0] > 1 if sizes.keep else levels_ref[0] > 0
+    begin = 1 if sizes.keep else 0
+    again = levels_ref[0] > begin
 
     @pl.when(again)
     def _():
-        prepare_tokens(sizes, table_ref, place_ref, attn_ref, vec_ref, table_t, place_t, w_kv, vec_t)
-
-    counts[...] = jnp.zeros_like(counts)
-    d_table_ref[...] = jnp.zeros_like(d_table_ref)
-    d_place_ref[...] = jnp.zeros_like(d_place_ref)
-    d_attn_ref[...] = jnp.zeros_like(d_attn_ref)
-    d_query_p[...] = jnp.zeros_like(d_query_p)
-    d_query_q[...] = jnp.zeros_like(d_query_q)
-    acc_gain[...] = jnp.zeros_like(acc_gain)
-    acc_shift[...] = jnp.zeros_like(acc_shift)
-    acc_value[...] = jnp.zeros_like(acc_value)
-
-    def one_level(level, carry_level):
-        for enc in range(2):
-            w_all = low16(attn_ref[0, enc, :, 128:384])
-
+        prepare_tokens(sizes, table_ref, place_ref, table_t, place_t)
+
+    for ref in (d_table_ref, d_place_ref, d_attn_ref, d_query_q, d_query_p, acc_gain, acc_shift, acc_value):
+        ref[...] = jnp.zeros_like(ref)
+
+    def ask_span(enc, step):
+        if enc == 0:
+            spot = pl.ds(step * 8, 8)
+            shape = (8 * count_q, 128)
+            found = [ref[spot, 0:count_q, :].reshape(shape) for ref in (query_ref, grad_ref, mixed_ref)]
+            lines = [jnp.broadcast_to(lse_ref[step * 8 + i, 1:2, :], (count_q, 128)) for i in range(8)]
+            lines = jnp.concatenate(lines, 0)
+            row = iota(lines.shape, 0) % count_q
+            lane = iota(lines.shape, 1)
+            lse = [
+                jnp.sum(jnp.where(lane == row + head * count_q, lines, 0.0), 1, keepdims=True)
+                for head in range(2)
+            ]
+            lse = jnp.concatenate(lse, 0)
+        else:
+            found = [ref[step, count_q:, :] for ref in (query_ref, grad_ref, mixed_ref)]
+            lines = jnp.broadcast_to(lse_ref[step, 0:1, :], (2 * count_p, 128))
+            lse = jnp.sum(jnp.where(iota(lines.shape, 1) == iota(lines.shape, 0), lines, 0.0), 1, keepdims=True)
+        return found + [lse]
+
+    def work(enc, steps, codes, scaleds, rates):
+        w_all = low16(attn_ref[0, enc, :, 128:384])
+        asked = [ask_span(enc, step) for step in steps]
+        made = [project(enc, scaled, vec_t, w_kv) for scaled in scaleds]
+        d_queries, d_kvs = ([], [])
+        for (query, grad, mixed, lse), code, (a_t, keys_t, values_t) in zip(asked, codes, made):
+            both = two_heads(query)
+            grads = two_heads(grad)
+            base = jnp.sum(
+                grads.astype(jnp.float32) * jnp.concatenate([mixed, mixed], 0).astype(jnp.float32),
+                1,
+                keepdims=True,
+            )
+            scores = dot(both, keys_t) * HEAD ** (-0.5)
+            mine = own_slots(code, query.shape[0])
+            probs = jnp.where(mine, jnp.exp(jnp.where(mine, scores, NEG) - lse), 0.0)
+            d_probs = dot(grads, values_t)
+            d_scores = low16(probs * (d_probs - base))
+            d_values = low16(dot_rows(grads, low16(probs)))
+            d_keys = low16(dot_rows(both, d_scores) * HEAD ** (-0.5))
+            d_queries.append(merge_heads(dot_last(d_scores, keys_t)) * HEAD ** (-0.5))
+            d_kvs.append(jnp.concatenate([d_keys, d_values], 0))
+        for step, d_query in zip(steps, d_queries):
+            if enc == 0:
+                d_query_q[step] += d_query
+            else:
+                d_query_p[step] += d_query
+        d_kv = jnp.concatenate(d_kvs, 1)
+        a_t = jnp.concatenate([part[0] for part in made], 1)
+        scaled = jnp.concatenate(scaleds, 1)
+        rate = jnp.concatenate(rates, 1)
+        code = jnp.concatenate(codes, 1)
+        width = code.shape[1]
+        d_attn_ref[enc] += dot_last(a_t, d_kv)
+        d_h = dot(w_all, d_kv)
+        fold = lambda values: sum(values[:, i * SPAN : (i + 1) * SPAN] for i in range(width // SPAN))
+        acc_value[enc] += fold(d_kv[128:].astype(jnp.float32))
+        acc_gain[enc] += fold(d_h * scaled)
+        acc_shift[enc] += fold(d_h)
+        d_scaled = d_h * vec_t[enc, :, 0:1]
+        center = d_scaled - jnp.mean(d_scaled, 0, keepdims=True)
+        slope = jnp.mean(d_scaled * scaled, 0, keepdims=True)
+        d_x = low16((center - scaled * slope) * rate)
+        rows = code >> 16
+        where = (code >> 8) & 255
+        chosen = hot(jnp.broadcast_to(where, (CHUNK, width)) == iota((CHUNK, width), 0))
+        d_place_ref[enc] += dot_last(d_x, chosen)
+        wide = jnp.broadcast_to(rows, (CHUNK, width))
+        for cut in range(sizes.padded // CHUNK):
+            spot = slice(cut * CHUNK, (cut + 1) * CHUNK)
+            chosen = hot(wide == iota((CHUNK, width), 0) + cut * CHUNK)
+            d_table_ref[:, spot] += dot_last(d_x, chosen)
+
+    for enc in range(2):
+        if sizes.keep:
+
+            def kept_spans(turn, carry):
+                steps = [turn * UNROLL + u for u in range(UNROLL)]
+                ats = [s if enc == 0 else sizes.steps[0] + s for s in steps]
+                work(
+                    enc,
+                    steps,
+                    [entry_ref[at, 0:1, :] for at in ats],
+                    [kept_ref[at, 0:128, :] for at in ats],
+                    [kept_ref[at, 128:129, :] for at in ats],
+                )
+                return carry
+
+            lax.fori_loop(0, sizes.steps[enc] // UNROLL, kept_spans, 0)
+
+        def more_level(level, carry_level):
             def one_span(step, carry):
-                at = step if enc == 0 else sizes.steps[0] + step
-                again_span = functools.partial(
-                    gather_span, sizes, enc, step, level, first, raw_ref, table_t, place_t, entries, counts, scaled_ref
-                )
-                if sizes.keep:
-
-                    @pl.when(level == 0)
-                    def _():
-                        scaled_ref[...] = kept_ref[at]
-                        entries[...] = entry_ref[at]
-
-                    pl.when(level > 0)(again_span)
-                else:
-                    again_span()
-                scaled = scaled_ref[0:128, :]
-                a_t, keys_t, values_t = project(enc, scaled, vec_t, w_kv)
-                if enc == 0:
-                    query = jnp.concatenate([query_ref[step * 8 + i, 0:count_q, :] for i in range(8)], 0)
-                    grad = jnp.concatenate([grad_ref[step * 8 + i, 0:count_q, :] for i in range(8)], 0)
-                    mixed = jnp.concatenate([mixed_ref[step * 8 + i, 0:count_q, :] for i in range(8)], 0)
-                    pieces = []
-                    for head in range(2):
-                        for i in range(8):
-                            line = lse_ref[step * 8 + i]
-                            tall = jnp.transpose(
-                                jnp.concatenate([line, jnp.zeros((120, 128), jnp.float32)], 0)
-                            )
-                            pieces.append(tall[head * count_q : (head + 1) * count_q, 1:2])
-                    lse = jnp.concatenate(pieces, 0)
-                else:
-                    query = query_ref[step, count_q:, :]
-                    grad = grad_ref[step, count_q:, :]
-                    mixed = mixed_ref[step, count_q:, :]
-                    tall = jnp.transpose(
-                        jnp.concatenate([lse_ref[step], jnp.zeros((120, 128), jnp.float32)], 0)
-                    )
-                    lse = tall[0 : 2 * count_p, 0:1]
-                number = query.shape[0]
-                both = two_heads(query)
-                grads = two_heads(grad)
-                level_sum = jnp.sum(
-                    grads.astype(jnp.float32) * jnp.concatenate([mixed, mixed], 0).astype(jnp.float32),
-                    1,
-                    keepdims=True,
-                )
-                scores = dot(both, keys_t) * HEAD ** (-0.5)
-                seq = (entries[0:1, :] & 255) - 1
-                line = iota(scores.shape, 0)
-                line = jnp.where(line >= number, line - number, line)
-                mine = line == seq
-                probs = jnp.where(mine, jnp.exp(jnp.where(mine, scores, NEG) - lse), 0.0)
-                d_probs = dot(grads, values_t)
-                d_scores = low16(probs * (d_probs - level_sum))
-                d_values = low16(dot_rows(grads, low16(probs)))
-                d_keys = low16(dot_rows(both, d_scores) * HEAD ** (-0.5))
-                d_query = merge_heads(dot_last(d_scores, keys_t)) * HEAD ** (-0.5)
-                if enc == 0:
-                    d_query_q[step] += d_query
-                else:
-                    d_query_p[step] += d_query
-                d_kv = jnp.concatenate([d_keys, d_values], 0)
-                d_attn_ref[enc] += dot_last(a_t, d_kv)
-                acc_value[enc] += d_values.astype(jnp.float32)
-                d_h = dot(w_all, d_kv)
-                acc_gain[enc] += d_h * scaled
-                acc_shift[enc] += d_h
-                d_scaled = d_h * vec_t[enc, :, 0:1]
-                center = d_scaled - jnp.mean(d_scaled, 0, keepdims=True)
-                slope = jnp.mean(d_scaled * scaled, 0, keepdims=True)
-                d_x = low16((center - scaled * slope) * scaled_ref[128:129, :])
-                rows = entries[0:1, :] >> 16
-                where = (entries[0:1, :] >> 8) & 255
-                chosen = hot(jnp.broadcast_to(where, (CHUNK, SPAN)) == iota((CHUNK, SPAN), 0))
-                d_place_ref[enc] += dot_last(d_x, chosen)
-                wide = jnp.broadcast_to(rows, (CHUNK, SPAN))
-                for cut in range(sizes.padded // CHUNK):
-                    spot = slice(cut * CHUNK, (cut + 1) * CHUNK)
-                    chosen = hot(wide == iota((CHUNK, SPAN), 0) + cut * CHUNK)
-                    d_table_ref[:, spot] += dot_last(d_x, chosen)
+                code = pack_span(sizes, enc, step, level, first, raw_ref)[0]
+                scaled, rate = gather_span(sizes, enc, code, table_t, place_t)
+                work(enc, [step], [code], [scaled], [rate])
                 return carry
 
-            lax.fori_loop(0, sizes.steps[enc], one_span, 0)
-        return carry_level
-
-    lax.fori_loop(0, levels_ref[0], one_level, 0)
-
-    def give(step, carry):
-        for i in range(8):
-            d_query_ref[step * 8 + i, 0:count_q, :] = low16(
-                d_query_q[step][i * count_q : (i + 1) * count_q]
-            )
-        return carry
-
-    lax.fori_loop(0, sizes.steps[0], give, 0)
+            return lax.fori_loop(0, sizes.steps[enc], one_span, carry_level)
+
+        lax.fori_loop(begin, levels_ref[0], more_level, 0)
+
+    for step in range(sizes.steps[0]):
+        d_query_ref[step * 8 : step * 8 + 8, 0:count_q, :] = low16(d_query_q[step]).reshape(8, count_q, 128)
     d_query_ref[:, count_q:, :] = low16(d_query_p[...])
     for enc in range(2):
         for part, block in enumerate((d_place_ref, d_attn_ref)):
@@ -773,10 +819,11 @@
                     slice_ref.dtype
                 )
     d_vec_ref[...] = jnp.zeros_like(d_vec_ref)
+    same = iota((128, 128), 0) == iota((128, 128), 1)
     for enc in range(2):
         for row, acc in enumerate((acc_gain, acc_shift, acc_value)):
             tall = jnp.broadcast_to(jnp.sum(acc[enc], 1, keepdims=True), (128, 128))
-            d_vec_ref[enc * 4 + row : enc * 4 + row + 1, :] = jnp.transpose(tall)[0:1, :]
+            d_vec_ref[enc * 4 + row : enc * 4 + row + 1, :] = jnp.sum(jnp.where(same, tall, 0.0), 0, keepdims=True)
 
 
 def tokens_backward(sizes, levels, every, query, mixed, lse, grad, kept, entry, table, positions, attention, vectors):
@@ -819,8 +866,7 @@
 def pieces_of(depth):
     blocks = [(1, (enc,)) for enc in range(2)] + [(2, (enc,)) for enc in range(2)]
     blocks += [(3, (enc, side)) for enc in range(2) for side in range(2)]
-    blocks += [(4, (enc,)) for enc in range(2)]
-    return blocks
+    return blocks + [(4, ())]
 
 
 def square_sum(values):
@@ -876,6 +922,7 @@
     spread_wait(many, me, pairs, send, recv, 3)
 
     first_sum = jnp.sum(first_all[...], 0)
+    g_vec[...] = d_mid[...]
     first = me * depth
     table_t[...] = d_table_ref[...]
     blocks = slice_all[...].astype(jnp.float32).reshape(8, 128, 128)
@@ -888,8 +935,8 @@
         center = x - jnp.mean(x, -1, keepdims=True)
         rate = lax.rsqrt(jnp.mean(center * center, -1, keepdims=True) + NORM_EPS)
         scaled = center * rate
-        gain = vec_ref[0, enc, 0:1, :]
-        a_low = low16(scaled * gain + vec_ref[0, enc, 1:2, :])
+        gain = vector_row(vec_ref, enc, 0)
+        a_low = low16(scaled * gain + vector_row(vec_ref, enc, 1))
         xa = xa_q if enc == 0 else xa_p
         d_h = xa[...] + dot_last(d_query, low16(attn_ref[0, enc, :, 0:128]))
         d_scaled = d_h * gain
@@ -902,11 +949,11 @@
         g_attn[enc, :, 128:256] = blocks[enc * 4 + 2]
         g_attn[enc, :, 256:384] = blocks[enc * 4 + 3]
         g_attn[enc, :, 384:512] = d_out[enc]
-        g_vec[enc] = d_mid[enc]
-        g_vec[enc, 0:1, :] = first_sum[enc * 4 : enc * 4 + 1] + jnp.sum(d_h * scaled, 0, keepdims=True)
-        g_vec[enc, 1:2, :] = first_sum[enc * 4 + 1 : enc * 4 + 2] + jnp.sum(d_h, 0, keepdims=True)
-        g_vec[enc, 2:3, :] = jnp.sum(d_query.astype(jnp.float32), 0, keepdims=True)
-        g_vec[enc, 3:4, :] = first_sum[enc * 4 + 2 : enc * 4 + 3]
+        spot = slice(enc, enc + 1)
+        g_vec[0, spot, :] = first_sum[enc * 4 : enc * 4 + 1] + jnp.sum(d_h * scaled, 0, keepdims=True)
+        g_vec[1, spot, :] = first_sum[enc * 4 + 1 : enc * 4 + 2] + jnp.sum(d_h, 0, keepdims=True)
+        g_vec[2, spot, :] = jnp.sum(d_query.astype(jnp.float32), 0, keepdims=True)
+        g_vec[3, spot, :] = first_sum[enc * 4 + 2 : enc * 4 + 3]
         if enc == 0:
             columns = [
                 part
@@ -925,11 +972,13 @@
         for cut in range(sizes.padded // CHUNK):
             chosen = hot(wide == iota((number, CHUNK), 1) + cut * CHUNK)
             table_t[:, cut * CHUNK : (cut + 1) * CHUNK] += dot_rows(d_low, chosen)
-        rest += square_sum(g_place[enc]) + square_sum(g_attn[enc]) + square_sum(g_vec[enc])
+        rest += square_sum(g_place[enc]) + square_sum(g_attn[enc])
         rest += square_sum(d_ffn[enc, 0]) + square_sum(d_ffn[enc, 1])
     for cut in range(0, depth, 128):
         top = min(cut + 128, depth)
         g_word[cut:top, :] = jnp.transpose(table_t[:, cut : cut + 128])[0 : top - cut]
+    small = jnp.sum(g_vec[...] * g_vec[...], 0)
+    rest += jnp.sum(jnp.sum(small, 0, keepdims=True), 1, keepdims=True)
     tile[...] = jnp.broadcast_to(square_sum(table_t[...]), (8, 128))
     pairs = [(lambda peer: tile, scalar_all)]
     spread_start(many, me, pairs, send, recv, 5)
@@ -1002,7 +1051,7 @@
         functools.partial(finish_kernel, sizes),
         out_shape=tuple(
             jax.ShapeDtypeStruct(shape, f32)
-            for shape in [(8, 128), shapes[0], shapes[1], shapes[2], (2, 16, 128)] + shapes
+            for shape in [(8, 128), shapes[0], shapes[1], shapes[2], (16, 2, 128)] + shapes
         ),
         in_specs=[vm] * len(inputs) + [hbm] * 20,
         out_specs=[vm] * 10,
@@ -1114,6 +1163,265 @@
         name="make_outputs",
     )(norm, grads[4], *flat)
     return [[got[kind * 5 + j] for kind in kinds] for j in range(5)]
+
+
+def square_norm(values):
+    center = values - jnp.mean(values, -1, keepdims=True)
+    rate = lax.rsqrt(jnp.mean(center * center, -1, keepdims=True) + NORM_EPS)
+    return center * rate, rate
+
+
+def norm_back(d_scaled, scaled, rate):
+    slope = jnp.mean(d_scaled * scaled, -1, keepdims=True)
+    return (d_scaled - jnp.mean(d_scaled, -1, keepdims=True) - scaled * slope) * rate
+
+
+def total_of(values):
+    return jnp.sum(jnp.sum(values, 0, keepdims=True), 1, keepdims=True)
+
+
+def score_terms(scores, drop, target, weight, count, axis):
+    masked = jnp.where(drop, MASKED, scores)
+    top = jnp.max(masked, axis, keepdims=True)
+    expo = jnp.exp(masked - top)
+    total = jnp.sum(expo, axis, keepdims=True)
+    picked = jnp.sum(jnp.where(target, scores, 0.0), axis, keepdims=True)
+    loss = total_of(weight * (top + jnp.log(total) - picked))
+    grad = low16((weight / count) * (expo / total - jnp.where(target, 1.0, 0.0)))
+    return grad, loss
+
+
+GELU_A = math.sqrt(2.0 / math.pi)
+GELU_B = 0.044715
+
+
+def class_kernel(
+    sizes,
+    rows_ref,
+    mixed_ref,
+    raw_ref,
+    place_ref,
+    attn_ref,
+    ffn_ref,
+    vec_ref,
+    grad_ref,
+    xa_q,
+    xa_p,
+    d_out,
+    d_ffn,
+    d_mid,
+    score_ref,
+    cls_ref,
+    scaled_a,
+    rate_a,
+    scaled_f,
+    rate_f,
+    pre_ref,
+    act_ref,
+    low_ref,
+    flag_ref,
+):
+    many = sizes.many
+    counts = sizes.count
+    totals = (many * counts[0], many * counts[1])
+    chunk = totals[0]
+    parts = [(0, 0, 0)] + [(1, at, totals[0] + at) for at in range(0, totals[1], chunk)]
+
+    def held(ref, enc, at):
+        each = counts[enc]
+        low = 0 if enc == 0 else counts[0]
+        return ref[at // each : (at + chunk) // each, low : low + each, :].reshape(chunk, 128)
+
+    def weights(enc):
+        return (
+            low16(attn_ref[0, enc, :, 384:512]),
+            low16(ffn_ref[0, enc, 0]),
+            low16(ffn_ref[0, enc, 1]),
+        )
+
+    for enc, at, spot in parts:
+        w_out, w_up, w_down = weights(enc)
+        row = functools.partial(vector_row, vec_ref, enc)
+        here = slice(spot, spot + chunk)
+        x = held(rows_ref, enc, at).astype(jnp.float32) + place_ref[0, enc, 0:1, :]
+        h_embed = norm_rows(x, row(0), row(1))
+        scaled, rate = square_norm(h_embed + (dot(held(mixed_ref, enc, at), w_out) + row(4)))
+        scaled_a[here, :] = scaled
+        rate_a[here, :] = jnp.broadcast_to(rate, (chunk, 128))
+        h_attn = scaled * row(5) + row(6)
+        h_low = low16(h_attn)
+        low_ref[here, :] = h_low
+        pre = dot(h_low, w_up) + jnp.concatenate([row(10), row(11), row(12), row(13)], 1)
+        pre_ref[here, :] = pre
+        act = low16(0.5 * pre * (1.0 + jnp.tanh(GELU_A * (pre + GELU_B * (pre * pre * pre)))))
+        act_ref[here, :] = act
+        scaled, rate = square_norm(h_attn + (dot_last(act, w_down) + row(7)))
+        scaled_f[here, :] = scaled
+        rate_f[here, :] = jnp.broadcast_to(rate, (chunk, 128))
+        cls_ref[here, :] = low16(scaled * row(8) + row(9))
+
+    every_q = cls_ref[0 : totals[0], :]
+    every_p = cls_ref[totals[0] :, :]
+    flag_ref[...] = jnp.zeros_like(flag_ref)
+    for peer in range(many):
+        flag_ref[peer : peer + 1, :] = raw_ref[peer, RAW_Q:RAW_ROWS, :].astype(jnp.float32)[8:9]
+    turned = jnp.transpose(flag_ref[...])
+
+    def column(low, each):
+        tall = jnp.concatenate([turned[low : low + each]] * many, 0)
+        at = iota(tall.shape, 1) == iota(tall.shape, 0) // each
+        return jnp.sum(jnp.where(at, tall, 0.0), 1, keepdims=True)
+
+    keys_q = column(0, counts[0])
+    valid = column(counts[0], counts[0])
+    keys_p = column(2 * counts[0], counts[1])
+    hot_q = hot(jnp.broadcast_to(keys_q, (totals[0], 128)) == iota((totals[0], 128), 1).astype(jnp.float32))
+    hot_p = hot(jnp.broadcast_to(keys_p, (totals[1], 128)) == iota((totals[1], 128), 1).astype(jnp.float32))
+    same = dot_last(hot_q, hot_p) > 0.5
+    count = jnp.maximum(total_of(valid), 1.0)
+    scale = 128 ** (-0.5)
+    scores = dot_last(every_q, every_p) * scale
+    index_q = iota(scores.shape, 0)
+    index_p = iota(scores.shape, 1)
+    target_qp = index_p == 2 * index_q
+    target_pq = index_p // 2 == index_q
+    grad_qp, loss_qp = score_terms(scores, same & ~target_qp, target_qp, valid, count, 1)
+    drop_pq = (same | (jnp.broadcast_to(valid, scores.shape) == 0.0)) & ~target_pq
+    weight_p = jnp.sum(jnp.where(target_qp, jnp.broadcast_to(valid, scores.shape), 0.0), 0, keepdims=True)
+    grad_pq, loss_pq = score_terms(scores, drop_pq, target_pq, weight_p, count, 0)
+    lane = iota((8, 128), 1)
+    score_ref[...] = jnp.where(lane == 0, loss_qp + loss_pq, count)
+    d_q = (dot(grad_qp, every_p) + dot(grad_pq, every_p)) * scale
+    d_p = (dot_rows(grad_pq, every_q) + dot_rows(grad_qp, every_q)) * scale
+
+    d_mid[...] = jnp.zeros_like(d_mid)
+    d_out[...] = jnp.zeros_like(d_out)
+    d_ffn[...] = jnp.zeros_like(d_ffn)
+    for enc, at, spot in parts:
+        w_out, w_up, w_down = weights(enc)
+        row = functools.partial(vector_row, vec_ref, enc)
+        here = slice(spot, spot + chunk)
+
+        def add(index, values):
+            d_mid[index, enc : enc + 1, :] += jnp.sum(values, 0, keepdims=True)
+
+        d_cls = d_q if enc == 0 else d_p[at : at + chunk]
+        scaled = scaled_f[here, :]
+        add(8, d_cls * scaled)
+        add(9, d_cls)
+        d_x_ffn = norm_back(d_cls * row(8), scaled, rate_f[here, :])
+        d_branch = low16(d_x_ffn)
+        add(7, d_branch.astype(jnp.float32))
+        d_ffn[enc, 1] += dot_rows(d_branch, act_ref[here, :])
+        d_act = dot(d_branch, w_down)
+        pre = pre_ref[here, :]
+        square = pre * pre
+        bend = jnp.tanh(GELU_A * (pre + GELU_B * (square * pre)))
+        slope = 0.5 * (1.0 + bend) + (0.5 * GELU_A) * pre * (1.0 - bend * bend) * (
+            1.0 + (3.0 * GELU_B) * square
+        )
+        d_pre = low16(slope * d_act)
+        up_bias = jnp.sum(d_pre.astype(jnp.float32), 0, keepdims=True)
+        for cut in range(4):
+            d_mid[10 + cut, enc : enc + 1, :] += up_bias[:, cut * 128 : (cut + 1) * 128]
+        d_ffn[enc, 0] += dot_rows(low_ref[here, :], d_pre)
+        d_h = d_x_ffn + dot_last(d_pre, w_up)
+        scaled = scaled_a[here, :]
+        add(5, d_h * scaled)
+        add(6, d_h)
+        d_x = norm_back(d_h * row(5), scaled, rate_a[here, :])
+        if enc == 0:
+            xa_q[...] = d_x
+        else:
+            xa_p[at : at + chunk, :] = d_x
+        d_proj = low16(d_x)
+        add(4, d_proj.astype(jnp.float32))
+        d_out[enc] += dot_rows(held(mixed_ref, enc, at), d_proj)
+        d_mixed = low16(dot_last(d_proj, w_out))
+        each = counts[enc]
+        low = 0 if enc == 0 else counts[0]
+        grad_ref[at // each : (at + chunk) // each, low : low + each, :] = d_mixed.reshape(
+            chunk // each, each, 128
+        )
+
+
+def class_stage(sizes, rows, mixed, every, positions, attention, feedforward, vectors):
+    many = sizes.many
+    n_q, n_p = (many * sizes.count[0], many * sizes.count[1])
+    both = n_q + n_p
+    f32 = jnp.float32
+    return local_call(
+        functools.partial(class_kernel, sizes),
+        (
+            jax.ShapeDtypeStruct((many, sum(sizes.count), 128), jnp.bfloat16),
+            jax.ShapeDtypeStruct((n_q, 128), f32),
+            jax.ShapeDtypeStruct((n_p, 128), f32),
+            jax.ShapeDtypeStruct((2, 128, 128), f32),
+            jax.ShapeDtypeStruct((2, 2, 128, 512), f32),
+            jax.ShapeDtypeStruct((16, 2, 128), f32),
+            jax.ShapeDtypeStruct((8, 128), f32),
+        ),
+        (rows, mixed, every, positions, attention, feedforward, vectors),
+        [
+            pltpu.VMEM((both, 128), jnp.bfloat16),
+            pltpu.VMEM((both, 128), f32),
+            pltpu.VMEM((both, 128), f32),
+            pltpu.VMEM((both, 128), f32),
+            pltpu.VMEM((both, 128), f32),
+            pltpu.VMEM((both, 512), f32),
+            pltpu.VMEM((both, 512), jnp.bfloat16),
+            pltpu.VMEM((both, 128), jnp.bfloat16),
+            pltpu.VMEM((128, 128), f32),
+        ],
+        "class_stage",
+    )
+
+
+def class_stage_large(sizes, rows_all, mixed_all, every, positions, attention, feedforward, vectors):
+    many = sizes.many
+    count_q, count_p = sizes.count
+    counts = sizes.count
+    width = rows_all.shape[2]
+    flags_all = every[:, RAW_FLAGS, :].astype(jnp.int32)
+    keys_q = flags_all[:, :count_q].reshape(-1)
+    valid_all = flags_all[:, count_q : 2 * count_q].reshape(-1)
+    keys_p = flags_all[:, 2 * count_q : 2 * count_q + count_p].reshape(-1)
+    cuts = ((0, count_q), (count_q, count_q + count_p))
+    cls, class_kept, mixes = ([], [], [])
+    for enc in range(2):
+        low, high = cuts[enc]
+        rows = rows_all[:, low:high].reshape(-1, width)
+        mixed = mixed_all[:, low:high].reshape(-1, width)
+        low_cls, kept_cls = class_forward(
+            rows, mixed, positions[0, enc], attention[0, enc], feedforward[0, enc], vectors[0, :, enc]
+        )
+        cls.append(low_cls)
+        class_kept.append(kept_cls)
+        mixes.append(mixed)
+    d_q, d_p, loss_total, count = score_stage(cls[0], cls[1], keys_q, keys_p, valid_all)
+    d_cls = (d_q, d_p)
+    grads, xas, outs, ffns, mids = ([], [], [], [], [])
+    for enc in range(2):
+        d_mixed, d_x_attn, d_w_out, d_ffn, rows_mid, d_up_bias = class_backward(
+            class_kept[enc], mixes[enc], attention[0, enc], feedforward[0, enc], vectors[0, :, enc], d_cls[enc]
+        )
+        grads.append(d_mixed.reshape(many, counts[enc], width))
+        xas.append(d_x_attn)
+        outs.append(d_w_out)
+        ffns.append(d_ffn)
+        mid = jnp.concatenate([jnp.stack(list(rows_mid)), d_up_bias.reshape(-1, width)])
+        mids.append(jnp.pad(mid, ((4, 2), (0, 0))))
+    lane = jnp.arange(128)[None, :]
+    score = jnp.broadcast_to(jnp.where(lane == 0, loss_total, count), (8, 128))
+    return (
+        jnp.concatenate(grads, 1),
+        xas[0],
+        xas[1],
+        jnp.stack(outs),
+        jnp.stack(ffns),
+        jnp.stack(mids, 1),
+        score,
+    )
 
 
 def class_forward(rows, mixed, place, attn_w, ffn_w, vec):
@@ -1219,76 +1527,36 @@
     feedforward_outer,
     vectors_outer,
 ):
-    width = word_table.shape[2]
     many = lax.axis_size("dp")
-    count_q, seq_q = question_ids.shape
-    count_p, seq_p = passage_ids.shape
-    counts = (count_q, count_p)
+    count_q = question_ids.shape[0]
+    count_p = passage_ids.shape[0]
     table = word_table[0]
     sizes = Sizes(many, count_q, count_p, table.shape[0])
-    ids_q = jnp.where(jnp.arange(seq_q)[None, :] < question_lengths[:, None], question_ids, -1)
-    ids_p = jnp.where(jnp.arange(seq_p)[None, :] < passage_lengths[:, None], passage_ids, -1)
-    half = count_q // 2
-    flags = jnp.concatenate([question_keys, question_valid, passage_keys])
-    flags = jnp.pad(flags, (0, 8 * 128 - flags.size)).reshape(8, 128)
-    raw = jnp.concatenate(
-        [
-            ids_p[:, :128],
-            ids_p[:, 128:],
-            jnp.concatenate([ids_q[:half], ids_q[half:]], 1),
-            flags,
-        ]
-    ).astype(jnp.int16)
-    every, class_rows = exchange_rows(many, count_q, count_p, raw, table)
-    flags_all = every[:, RAW_FLAGS, :].astype(jnp.int32)
-    keys_q = flags_all[:, :count_q].reshape(-1)
-    valid_all = flags_all[:, count_q : 2 * count_q].reshape(-1)
-    keys_p = flags_all[:, 2 * count_q : 2 * count_q + count_p].reshape(-1)
+    swap = lambda values: jnp.swapaxes(values, -3, -2)
+    vectors, vectors_first, vectors_second, vectors_anchor, vectors_outer = (
+        swap(v) for v in (vectors, vectors_first, vectors_second, vectors_anchor, vectors_outer)
+    )
+    every, class_rows = exchange_rows(
+        many,
+        question_ids,
+        passage_ids,
+        question_lengths,
+        passage_lengths,
+        question_keys,
+        question_valid,
+        passage_keys,
+        table,
+    )
     part, lse_part, query, kept, entry, levels = tokens_forward(
         sizes, every, class_rows, table, positions, attention, vectors
     )
     mixed_all, lse_all = exchange_mixed(sizes, part, lse_part)
-    cuts = ((0, count_q), (count_q, count_q + count_p))
-    cls, class_kept, mixes, class_x = ([], [], [], [])
-    for enc in range(2):
-        low, high = cuts[enc]
-        rows = class_rows[:, low:high].reshape(-1, width)
-        mixed = mixed_all[:, low:high].reshape(-1, width)
-        low_cls, kept_cls = class_forward(
-            rows, mixed, positions[0, enc], attention[0, enc], feedforward[0, enc], vectors[0, enc]
-        )
-        cls.append(low_cls)
-        class_kept.append(kept_cls)
-        mixes.append(mixed)
-        class_x.append(rows.astype(jnp.float32) + positions[0, enc, :1])
-    d_q, d_p, loss_total, count = score_stage(cls[0], cls[1], keys_q, keys_p, valid_all)
-    d_cls = (d_q, d_p)
-    finals, grad_parts, firsts_x = ([], [], [])
-    for enc in range(2):
-        d_mixed, d_x_attn, d_w_out, d_ffn, rows_mid, d_up_bias = class_backward(
-            class_kept[enc], mixes[enc], attention[0, enc], feedforward[0, enc], vectors[0, enc], d_cls[enc]
-        )
-        grad_parts.append(d_mixed.reshape(many, counts[enc], width))
-        firsts_x.append(d_x_attn)
-        finals.append((d_w_out, d_ffn, rows_mid, d_up_bias))
-    grad_all = jnp.concatenate(grad_parts, 1)
+    stage = class_stage if many * count_q <= 512 else class_stage_large
+    grad_all, xa_q, xa_p, d_out, d_ffn, d_mid, score = stage(
+        sizes, class_rows, mixed_all, every, positions, attention, feedforward, vectors
+    )
     d_query, d_table_t, slices, d_first = tokens_backward(
         sizes, levels, every, query, mixed_all, lse_all, grad_all, kept, entry, table, positions, attention, vectors
-    )
-    d_out = jnp.stack([finals[0][0], finals[1][0]])
-    d_ffn = jnp.stack([finals[0][1], finals[1][1]])
-    d_mid = jnp.stack(
-        [
-            jnp.concatenate(
-                [
-                    jnp.zeros((4, width), jnp.float32),
-                    jnp.stack(list(part[2])),
-                    part[3].reshape(-1, width),
-                    jnp.zeros((2, width), jnp.float32),
-                ]
-            )
-            for part in finals
-        ]
     )
     weights = (word_table, positions, attention, feedforward, vectors)
     firsts = (word_first, positions_first, attention_first, feedforward_first, vectors_first)
@@ -1303,8 +1571,8 @@
         d_table_t,
         class_rows,
         every,
-        firsts_x[0],
-        firsts_x[1],
+        xa_q,
+        xa_p,
         d_out,
         d_ffn,
         d_mid,
@@ -1313,10 +1581,15 @@
     )
     norm = done[0]
     grads = (done[1], done[2], done[3], d_ffn, done[4])
-    first_new, second_new, averages, outer_next, weight_next = make_outputs(
+    made = make_outputs(
         norm, grads, firsts, seconds, anchors, outers, done[5:10], lax.axis_size("grp")
     )
+    first_new, second_new, averages, outer_next, weight_next = (
+        part[:4] + [swap(part[4])] for part in made
+    )
     norm = norm[0, 0]
+    loss_total = score[0, 0]
+    count = score[0, 1]
     return (
         loss_total.reshape(1),
         count.reshape(1),

time: 271 us -> 185 us (0.68)
  other arithmetic: 25.9 us -> 0 us
  Pallas kernels: 206 us -> 181 us
  local copies, waits for them, and re-layouts: 20 us -> 2.53 us
  matrix products: 11.7 us -> 0 us
  between operations: 5.42 us -> 0.89 us
    pallas_call x2 -> x3, Pallas kernels: 92.8 us -> 72.3 us  [local_call(): pl.pallas_call(kernel, out_shape=out_shape, in_specs=[sm if i in smem_in...]
    unnamed x40 -> x0, local copies, waits for them, and re-layouts: 13.5 us -> none
    dot_general x23 -> x0, matrix products: 11.7 us -> none  [the longest x8 4.92 us: dot_rows(): lax.dot_general(left, right, CONTRACT_ROWS, preferred_element_type=jnp.fl...]
    reduce_sum x19 -> x0, other arithmetic: 10.2 us -> none  [the longest x6 4.56 us: layer_norm(): center = values - jnp.mean(values, -1, keepdims=True)]
    another operation x11 -> x0, other arithmetic: 7.28 us -> none
    pallas_call x1, Pallas kernels: 35.9 us -> 31.7 us  [exchange_rows(): pl.pallas_call(functools.partial(rows_kernel, many), out_shape=(jax.Shape...]
where the time goes in v1:
time: 185 us
  Pallas kernels  181 us (98%)
  local copies, waits for them, and re-layouts  2.53 us (1%)
    pallas_call x3, Pallas kernels, local_call(): pl.pallas_call(kernel, out_shape=out_shape, in_specs=[sm if i in smem_in...  72.3 us
    pallas_call x1, Pallas kernels, finish(): pl.pallas_call(functools.partial(finish_kernel, sizes), out_shape=tuple((...  47.4 us
    pallas_call x1, Pallas kernels, exchange_rows(): pl.pallas_call(functools.partial(rows_kernel, many), out_shape=(jax.Shape...  31.7 us
    pallas_call x1, Pallas kernels, remote_call(): pl.pallas_call(kernel, out_shape=out_shape, in_specs=[pl.BlockSpec(memory...  17.6 us
    pallas_call x1, Pallas kernels, make_outputs(): pl.pallas_call(functools.partial(outputs_kernel, anchors[0].shape[0], gro...  12.4 us

profile of v1, /device:TPU:0, one launch (start us, length us, event | category | flops | bytes accessed | tf_op | source)
XLA Modules:
  0.0 184.8 jit_solution(13710037265675375185)
XLA Ops:
  0.7 31.7 %exchange_rows.1 = (s16[16,80,128]{2,1,0:T(8,128)(2,1)}, bf16[16,48,128]{2,1,0:T(8,128)(2,1)}) custom-call(s32[16,64]{1,0:T(8,128)} %question_ref.1, s32[32,256]{1,0:T(8,128)} %passage_ref.1, s32[16]{0:T(128)} %length_q.1, s32[32]{0:T(128)} %length_p.1, s32[16]{0:T(128)} %key_q.1, s32[16]{0:T(128)} %valid_q.1, s32[32]{0:T(128)} %key_p.1, f32[1920,128]{1,0:T(8,128)} %bitcast.15), custom_call_target="tpu_custom_call" | custom-call | tf_op jit(solution)/shard_map/exchange_rows/pallas_call | solution.py:230
  32.4 34.5 %tokens_forward.1 = (bf16[16,48,128]{2,1,0:T(8,128)(2,1)}, f32[16,8,128]{2,1,0:T(8,128)}, bf16[16,48,128]{2,1,0:T(8,128)(2,1)}, f32[19,136,512]{2,1,0:T(8,128)}, s32[19,8,512]{2,1,0:T(8,128)}, /*index=5*/s32[1]{0:T(128)}) custom-call(s16[16,80,128]{2,1,0:T(8,128)(2,1)} %get-tuple-element.85.raw_ref.refs_5_, ...), custom_call_target="tpu_custom_call" | custom-call | tf_op jit(solution)/shard_map/tokens_forward/pallas_call | solution.py:550
  66.9 17.6 %exchange_mixed.1 = (bf16[16,48,128]{2,1,0:T(8,128)(2,1)}, f32[16,8,128]{2,1,0:T(8,128)}) custom-call(bf16[16,48,128]{2,1,0:T(8,128)(2,1)} %get-tuple-element.86.part_ref, f32[16,8,128]{2,1,0:T(8,128)} %get-tuple-element.87.lse_ref), custom_call_target="tpu_custom_call" | custom-call | tf_op jit(solution)/shard_map/exchange_mixed/pallas_call | solution.py:631
  84.5 8.2 %class_stage.1 = (bf16[16,48,128]{2,1,0:T(8,128)(2,1)}, f32[256,128]{1,0:T(8,128)}, f32[512,128]{1,0:T(8,128)}, f32[2,128,128]{2,1,0:T(8,128)}, f32[2,2,128,512]...) custom-call(bf16[16,48,128]{2,1,0:T(8,128)(2,1)} %get-tuple-element.84.rows_ref.refs_4_, ...), custom_call_target="tpu_custom_call" | custom-call | tf_op jit(solution)/shard_map/class_stage/pallas_call | solution.py:550
  92.7 29.6 %tokens_backward.1 = (bf16[16,48,128]{2,1,0:T(8,128)(2,1)}, f32[128,2048]{1,0:T(8,128)}, bf16[2,4,128,128]{3,2,1,0:T(8,128)(2,1)}, f32[8,128]{1,0:T(8,128)}) custom-call(s32[1]{0:T(128)} %get-tuple-element.90.levels_ref, s16[16,80,128]{2,1,0:T(8,128)(2,1)} %get-tuple-element.85.raw_ref.refs_5_, bf16[16,48,128]{2,1,0:T(8,128)(2,1)} %get-tuple-element.91.query_ref, ...), custom_call_target="tpu_custom_call" | custom-call | tf_op jit(solution)/shard_map/tokens_backward/pallas_call | solution.py:550
  122.2 1.3 fusion
  123.6 47.4 %finish.1 = (f32[8,128]{1,0:T(8,128)}, f32[1920,128]{1,0:T(8,128)}, f32[2,256,128]{2,1,0:T(8,128)}, f32[2,128,512]{2,1,0:T(8,128)}, f32[16,2,128]{2,1,0:T(2,128)...) custom-call(bf16[16,48,128]{2,1,0:T(8,128)(2,1)} %get-tuple-element., ...), custom_call_target="tpu_custom_call" | custom-call | tf_op jit(solution)/shard_map/finish/pallas_call | solution.py:1050
  170.9 1.2 slice.11
  172.1 12.4 %make_outputs.1 = (f32[1,1920,128]{2,1,0:T(8,128)}, f32[1,1920,128]{2,1,0:T(8,128)}, f32[1920,128]{1,0:T(8,128)}, f32[1920,128]{1,0:T(8,128)}, f32[1,1920,128]{2...) custom-call(f32[8,128]{1,0:T(8,128)} %get-tuple-element.105.refs_0_,, ...), custom_call_target="tpu_custom_call" | custom-call | tf_op jit(solution)/shard_map/make_outputs/pallas_call | solution.py:1154
